TPU v7x, 128 devices: a whole 4x4x4 slice. The times are simulated.
128 devices in a mesh: lon: 8 (over z_lo, x), lat: 16 (over z_hi, y, core).
Axes of the slice: x: 4, y: 4, z: 4 (z_hi: 2, z_lo: 2; z = z_hi * 2 + z_lo), core: 2. Of those that a mesh axis runs over, the one named last changes fastest.
Arguments:
- source_field: float32 [4, 768, 4096], P(None, 'lat', 'lon'), may hold values from -6 to 6
- helm_diag: float32 [4, 768, 4096], P(None, 'lat', 'lon'), may hold values from 0.05 to 1
- vertical: float32 [4], replicated, may hold values from 0.25 to 2
- cubic_band: float32 [8, 4], replicated, may hold values from 0.1 to 0.5
- lat_offset: int32 [768], P('lat'), may hold values from -8 to 8, as said below
- zonal_shift: int32 [768], P('lat'), may hold values from -16 to 15
- row_class: int32 [768], P('lat'), may hold values from 0 to 7
Outputs:
- departure: float32 [4, 768, 4096], P(None, 'lat', 'lon')
- solution: float32 [4, 768, 4096], P(None, 'lat', 'lon')
Inputs may be any that keep to these rules, and one draw needn't show every extreme that they name: j + lat_offset[j] lies within 0 to 767 for every row j.
All inputs are finite; a program needn't handle non-finite values.
Results may differ from a plain program's by a relative error of at most 0.0001.
Values sent between devices are 32-bit elements; how exact they have to be, the bound alone decides.
A program may use at most 192 MiB of HBM per device.

v0:
```python
from functools import partial

import jax
import jax.numpy as jnp
from jax import lax
from jax.sharding import PartitionSpec as P

DRIFT = 8
ITERS = 8


def with_halo(cells, sides, width, closed):
    for axis, dim in sides:
        count = lax.axis_size(axis)
        ends = count if closed else count - 1
        head = lax.slice_in_dim(cells, 0, width, axis=dim)
        tail = lax.slice_in_dim(cells, cells.shape[dim] - width, cells.shape[dim], axis=dim)
        cells = jnp.concatenate(
            [
                lax.ppermute(tail, axis, [(i, (i + 1) % count) for i in range(ends)]),
                cells,
                lax.ppermute(head, axis, [((i + 1) % count, i) for i in range(ends)]),
            ],
            axis=dim,
        )
    return cells


def shifted(x, axis, by):
    peers = lax.axis_size(axis)
    return lax.ppermute(x, axis, [(i, (i + by) % peers) for i in range(peers)])


def band_row(row_cells, begin_at, weights, length):
    window = lax.dynamic_slice_in_dim(row_cells, begin_at, length + 3, 1)
    summed = weights[0] * window[:, 0:length]
    summed = summed + weights[1] * window[:, 1 : length + 1]
    summed = summed + weights[2] * window[:, 2 : length + 2]
    summed = summed + weights[3] * window[:, 3 : length + 3]
    return summed


def finish(framed, remain, row_table, lon_cells):
    begins = lon_cells - 128 * remain - 1
    banded = jax.vmap(partial(band_row, length=lon_cells), in_axes=(1, 0, 0), out_axes=1)
    return banded(framed, begins, row_table)


def local_terms(values, helm_diag, vertical, east_west, north_south):
    stacked = jnp.pad(values, ((1, 1), (0, 0), (0, 0)))
    up_down = stacked[2:] + stacked[:-2]
    coupling = vertical[:, None, None]
    return (
        (4.0 + 2.0 * coupling + helm_diag) * values - (east_west + north_south) - coupling * up_down
    )


def operate(values, helm_diag, vertical):
    zonal = with_halo(values, (("lon", 2),), 1, True)
    meridional = with_halo(values, (("lat", 1),), 1, False)
    east_west = zonal[:, :, 2:] + zonal[:, :, :-2]
    north_south = meridional[:, 2:, :] + meridional[:, :-2, :]
    return local_terms(values, helm_diag, vertical, east_west, north_south)


def squares(residual):
    return lax.psum(jnp.sum(residual * residual), ("lon", "lat"))


def body(source_field, helm_diag, vertical, cubic_band, lat_offset, zonal_shift, row_class):
    levels, lat_rows, lon_cells = source_field.shape
    lon_count = lax.axis_size("lon")
    total_lon = lon_cells * lon_count
    blocks = jnp.mod(zonal_shift, total_lon // 128)
    row_table = jnp.dot(
        jax.nn.one_hot(row_class, cubic_band.shape[0], dtype=jnp.float32),
        cubic_band,
        precision=lax.Precision.HIGHEST,
    )
    padded = with_halo(source_field, (("lat", 1),), DRIFT, False)
    picked = jnp.take(padded, jnp.arange(lat_rows, dtype=jnp.int32) + DRIFT + lat_offset, axis=1)
    per_device = lon_cells // 128
    device_steps = (blocks // per_device)[None, :, None]
    remain = blocks % per_device

    def advance(counter, carry):
        current, result = carry
        current = shifted(current, "lon", 1)
        result = jnp.where(device_steps == counter, current, result)
        return (current, result)

    moved = lax.fori_loop(1, lon_count, advance, (picked, picked))[1]
    framed = with_halo(moved, (("lon", 2),), lon_cells, True)
    departure = finish(framed, remain, row_table, lon_cells)
    solution = jnp.zeros_like(departure)
    residual = departure
    direction = departure
    norm_now = squares(residual)
    for iteration in range(ITERS):
        applied = operate(direction, helm_diag, vertical)
        step_size = norm_now / lax.psum(jnp.sum(direction * applied), ("lon", "lat"))
        solution = solution + step_size * direction
        if iteration + 1 < ITERS:
            residual = residual - step_size * applied
            norm_next = squares(residual)
            direction = residual + norm_next / norm_now * direction
            norm_now = norm_next
    return (departure, solution)


def solution(mesh):
    return jax.shard_map(
        body,
        mesh=mesh,
        in_specs=(
            P(None, "lat", "lon"),
            P(None, "lat", "lon"),
            P(),
            P(),
            P("lat"),
            P("lat"),
            P("lat"),
        ),
        out_specs=(P(None, "lat", "lon"), P(None, "lat", "lon")),
        check_vma=False,
    )
```

profile of v0, /device:TPU:1, one launch (start us, length us, event | category | flops | bytes accessed | tf_op | source)
XLA Modules:
  0.0 1342.2 jit_solution(12595231336932468176)
XLA Ops:
  1.9 4.6 collective-permute-start.1
  13.4 81.9 %while.15 = (s32[]{:T(128)}, f32[4,48,512]{2,1,0:T(8,128)S(1)}, f32[4,48,512]{2,1,0:T(8,128)S(1)}, s32[1,48,1]{1,2,0:T(1,128)S(1)}, s32[]{:T(128)}) while((s32[]{:T(128)}, f32[4,48,512]{2,1,0:T(8,128)S(1)}, f32[4,48,512]{2,1,0:T(8,128)S(1)}, s32[1,48,1]{1,2,0:T(1,128)S(1)}, s32[]{:T(128)}) %tuple.77), condition=%wide.region_1.2_spmd, body=%wide.region_0.1_spmd.sunk | while | flops 98354 | bytes 3539337 | solution.py:92
  14.7 9.8 collective-permute-done
  24.7 11.8 collective-permute-done
  36.8 13.2 collective-permute-done
  50.2 12.4 collective-permute-done
  62.9 11.5 collective-permute-done
  74.6 10.5 collective-permute-done
  85.5 9.6 collective-permute-done
  95.3 4.1 collective-permute-start.4
  99.6 4.5 collective-permute-done.3
  104.2 23.5 %copy.216 = f32[4,48,1536]{0,1,2:T(8,128)} copy(f32[4,48,1536]{2,1,0:T(8,128)S(1)} %pad_maximum_fusion) | data formatting | bytes 2359296 | tf_op jit(solution)/shard_map/concatenate | solution.py:18
  127.7 27.3 %gather_fusion.1 = f32[48,4,515]{1,0,2:T(8,128)} fusion(f32[48,4,1536]{1,0,2:T(8,128)} %bitcast.26, s32[48]{0:T(128)S(1)} %get-tuple-element.139), kind=kCustom, calls=%fused_computation.1 | custom fusion | bytes 791616 | tf_op jit(solution)/shard_map/vmap()/gather | solution.py:35
  154.9 33.2 %fusion.72 = (f32[48,4,512]{1,0,2:T(8,128)}, f32[48,4,512]{1,0,2:T(8,128)}, f32[48,4,512]{1,0,2:T(8,128)}, f32[48,4,512]{1,0,2:T(8,128)}) fusion(f32[48,4,515]{1,0,2:T(8,128)} %gather_fusion.1), kind=kLoop, calls=%fused_computation.170 | loop fusion | bytes 3145728 | tf_op jit(solution)/shard_map/vmap()/slice | solution.py:36
  188.2 7.6 copy.221
  195.8 7.7 copy.222
  203.5 7.7 copy.223
  211.2 7.6 copy.224
  219.2 4.1 collective-permute-start.5
  223.4 7.6 collective-permute-start.7
  235.2 71.3 %all-reduce.9 = (f32[]{:T(128)}, f32[]{:T(128)}) all-reduce(f32[]{:T(128)} %get-tuple-element.105, f32[]{:T(128)} %get-tuple-element.104), channel_id=1, replica_groups=mesh['lon'=8,'lat'=16] {'lon','lat'}, use_global_device_ids=true, to_apply=%region_3.4 | all-reduce | flops 2 | bytes 16 | tf_op jit(solution)/shard_map/psum | solution.py:67
  308.4 62.7 %psum.114 = f32[]{:T(128)} all-reduce(f32[]{:T(128)} %multiply_reduce_fusion.12), channel_id=1, replica_groups=mesh['lon'=8,'lat'=16] {'lon','lat'}, use_global_device_ids=true, to_apply=%region_7.8 | all-reduce | flops 1 | bytes 8 | tf_op jit(solution)/shard_map/psum | solution.py:67
  374.9 3.1 collective-permute-start.12
  385.7 67.6 %psum.115 = f32[]{:T(128)} all-reduce(f32[]{:T(128)} %get-tuple-element.136), channel_id=1, replica_groups=mesh['lon'=8,'lat'=16] {'lon','lat'}, use_global_device_ids=true, to_apply=%region_9.10 | all-reduce | flops 1 | bytes 8 | tf_op jit(solution)/shard_map/psum | solution.py:101
  455.4 62.6 %psum.116 = f32[]{:T(128)} all-reduce(f32[]{:T(128)} %get-tuple-element.134), channel_id=1, replica_groups=mesh['lon'=8,'lat'=16] {'lon','lat'}, use_global_device_ids=true, to_apply=%region_11.12 | all-reduce | flops 1 | bytes 8 | tf_op jit(solution)/shard_map/psum | solution.py:67
  521.8 3.1 collective-permute-start.16
  529.4 3.9 collective-permute-done.14
  534.2 65.7 %psum.117 = f32[]{:T(128)} all-reduce(f32[]{:T(128)} %get-tuple-element.132), channel_id=1, replica_groups=mesh['lon'=8,'lat'=16] {'lon','lat'}, use_global_device_ids=true, to_apply=%region_13.14 | all-reduce | flops 1 | bytes 8 | tf_op jit(solution)/shard_map/psum | solution.py:101
  601.9 62.6 %psum.118 = f32[]{:T(128)} all-reduce(f32[]{:T(128)} %get-tuple-element.130), channel_id=1, replica_groups=mesh['lon'=8,'lat'=16] {'lon','lat'}, use_global_device_ids=true, to_apply=%region_15.16 | all-reduce | flops 1 | bytes 8 | tf_op jit(solution)/shard_map/psum | solution.py:67
  668.3 3.1 collective-permute-start.20
  675.9 3.6 collective-permute-done.18
  680.6 66.2 %psum.119 = f32[]{:T(128)} all-reduce(f32[]{:T(128)} %get-tuple-element.128), channel_id=1, replica_groups=mesh['lon'=8,'lat'=16] {'lon','lat'}, use_global_device_ids=true, to_apply=%region_17.18 | all-reduce | flops 1 | bytes 8 | tf_op jit(solution)/shard_map/psum | solution.py:101
  748.8 62.6 %psum.120 = f32[]{:T(128)} all-reduce(f32[]{:T(128)} %get-tuple-element.126), channel_id=1, replica_groups=mesh['lon'=8,'lat'=16] {'lon','lat'}, use_global_device_ids=true, to_apply=%region_19.20 | all-reduce | flops 1 | bytes 8 | tf_op jit(solution)/shard_map/psum | solution.py:67
  815.3 3.1 collective-permute-start.24
  822.9 3.6 collective-permute-done.22
  827.5 66.0 %psum.121 = f32[]{:T(128)} all-reduce(f32[]{:T(128)} %get-tuple-element.124), channel_id=1, replica_groups=mesh['lon'=8,'lat'=16] {'lon','lat'}, use_global_device_ids=true, to_apply=%region_21.22 | all-reduce | flops 1 | bytes 8 | tf_op jit(solution)/shard_map/psum | solution.py:101
  895.6 62.6 %psum.122 = f32[]{:T(128)} all-reduce(f32[]{:T(128)} %get-tuple-element.122), channel_id=1, replica_groups=mesh['lon'=8,'lat'=16] {'lon','lat'}, use_global_device_ids=true, to_apply=%region_23.24 | all-reduce | flops 1 | bytes 8 | tf_op jit(solution)/shard_map/psum | solution.py:67
  962.1 3.1 collective-permute-start.28
  969.7 3.6 collective-permute-done.26
  975.0 66.0 %psum.123 = f32[]{:T(128)} all-reduce(f32[]{:T(128)} %get-tuple-element.120), channel_id=1, replica_groups=mesh['lon'=8,'lat'=16] {'lon','lat'}, use_global_device_ids=true, to_apply=%region_25.26 | all-reduce | flops 1 | bytes 8 | tf_op jit(solution)/shard_map/psum | solution.py:101
  1044.0 62.6 %psum.124 = f32[]{:T(128)} all-reduce(f32[]{:T(128)} %get-tuple-element.118), channel_id=1, replica_groups=mesh['lon'=8,'lat'=16] {'lon','lat'}, use_global_device_ids=true, to_apply=%region_27.28 | all-reduce | flops 1 | bytes 8 | tf_op jit(solution)/shard_map/psum | solution.py:67
  1110.5 3.1 collective-permute-start.32
  1118.1 3.6 collective-permute-done.30
  1123.4 66.2 %psum.125 = f32[]{:T(128)} all-reduce(f32[]{:T(128)} %get-tuple-element.116), channel_id=1, replica_groups=mesh['lon'=8,'lat'=16] {'lon','lat'}, use_global_device_ids=true, to_apply=%region_29.30 | all-reduce | flops 1 | bytes 8 | tf_op jit(solution)/shard_map/psum | solution.py:101
  1192.7 62.6 %psum.126 = f32[]{:T(128)} all-reduce(f32[]{:T(128)} %multiply_reduce_fusion), channel_id=1, replica_groups=mesh['lon'=8,'lat'=16] {'lon','lat'}, use_global_device_ids=true, to_apply=%region_31.32 | all-reduce | flops 1 | bytes 8 | tf_op jit(solution)/shard_map/psum | solution.py:67
  1260.2 3.1 collective-permute-start.36
  1267.8 3.6 collective-permute-done.34
  1272.5 66.0 %psum.127 = f32[]{:T(128)} all-reduce(f32[]{:T(128)} %fusion.25), channel_id=1, replica_groups=mesh['lon'=8,'lat'=16] {'lon','lat'}, use_global_device_ids=true, to_apply=%region_33.34 | all-reduce | flops 1 | bytes 8 | tf_op jit(solution)/shard_map/psum | solution.py:101
  (151 shorter events, 86.1 us)
Async XLA Ops:
  0.6 98.8 %copy-start = (f32[8,4]{0,1:T(4,128)S(1)}, f32[8,4]{0,1:T(4,128)}, u32[]{:S(2)}) copy-start(f32[8,4]{0,1:T(4,128)} %param.12) | copy-start | bytes 388
  0.6 98.8 %copy-start.6 = (s32[48]{0:T(128)S(1)}, s32[48]{0:T(128)}, u32[]{:S(2)}) copy-start(s32[48]{0:T(128)} %param.15) | copy-start | bytes 580
  1.9 7.9 collective-permute-start.1
  6.5 5.6 collective-permute-start.2
  13.4 11.1 collective-permute-start
  24.6 11.9 collective-permute-start
  36.7 13.3 collective-permute-start
  50.1 12.5 collective-permute-start
  62.8 11.6 collective-permute-start
  74.5 10.6 collective-permute-start
  85.4 9.7 collective-permute-start
  95.3 8.8 collective-permute-start.3
  95.3 8.8 collective-permute-start.4
  203.5 30.6 %copy-start.2 = (f32[4,48,512]{2,1,0:T(8,128)S(1)}, f32[4,48,512]{2,1,0:T(8,128)}, u32[]{:S(2)}) copy-start(f32[4,48,512]{2,1,0:T(8,128)} %param.10) | copy-start | bytes 1179652
  219.0 1120.7 %copy-start.3 = (f32[4,48,512]{2,1,0:T(8,128)}, f32[4,48,512]{2,1,0:T(8,128)S(1)}, u32[]{:S(2)}) copy-start(f32[4,48,512]{2,1,0:T(8,128)S(1)} %add_bitcast_fusion) | copy-start | bytes 1179652
  219.2 13.8 %collective-permute-start.5 = (f32[4,48,1]{2,1,0:T(8,128)S(1)}, f32[4,48,1]{2,1,0:T(8,128)S(1)}, u32[]{:S(2)}, u32[]{:S(2)}) collective-permute-start(f32[4,48,1]{2,1,0:T(8,128)S(1)} %get-tuple-element.175), channel_id=1, source_target_pairs={{16,0},{32,16},{48,32},{64,48},{80,64},{96,80},{112,96},{0,112},{1... | collective-permute-start | bytes 2312 | tf_op jit(solution)/shard_map/ppermute | solution.py:22
  223.2 9.7 collective-permute-start.6
  223.4 9.6 collective-permute-start.7
  231.0 3.1 collective-permute-start.8
  372.4 12.2 collective-permute-start.11
  374.9 9.8 collective-permute-start.12
  378.1 6.5 collective-permute-start.10
  379.0 5.7 collective-permute-start.9
  519.3 13.9 %collective-permute-start.15 = (f32[4,1,512]{2,1,0:T(1,128)S(1)}, f32[4,1,512]{2,1,0:T(1,128)S(1)}, u32[]{:S(2)}, u32[]{:S(2)}) collective-permute-start(f32[4,1,512]{2,1,0:T(1,128)S(1)} %get-tuple-element.169), channel_id=1, source_target_pairs={{1,0},{2,1},{3,2},{4,3},{5,4},{6,5},{7,6},{8,7},{9,8},{10,9},{11,1... | collective-permute-start | bytes 24584 | tf_op jit(solution)/shard_map/ppermute | solution.py:22
  521.8 11.5 collective-permute-start.16
  525.0 4.4 collective-permute-start.13
  526.7 815.2 %copy-start.1 = (f32[8,4]{0,1:T(4,128)S(1)}, f32[8,4]{0,1:T(4,128)}, u32[]{:S(2)}) copy-start(f32[8,4]{0,1:T(4,128)} %param.12) | copy-start | bytes 388
  526.7 6.6 collective-permute-start.14
  665.9 13.7 %collective-permute-start.19 = (f32[4,1,512]{2,1,0:T(1,128)S(1)}, f32[4,1,512]{2,1,0:T(1,128)S(1)}, u32[]{:S(2)}, u32[]{:S(2)}) collective-permute-start(f32[4,1,512]{2,1,0:T(1,128)S(1)} %get-tuple-element.165), channel_id=1, source_target_pairs={{1,0},{2,1},{3,2},{4,3},{5,4},{6,5},{7,6},{8,7},{9,8},{10,9},{11,1... | collective-permute-start | bytes 24584 | tf_op jit(solution)/shard_map/ppermute | solution.py:22
  668.3 11.2 collective-permute-start.20
  671.6 4.4 collective-permute-start.17
  672.7 6.8 collective-permute-start.18
  812.9 13.7 %collective-permute-start.23 = (f32[4,1,512]{2,1,0:T(1,128)S(1)}, f32[4,1,512]{2,1,0:T(1,128)S(1)}, u32[]{:S(2)}, u32[]{:S(2)}) collective-permute-start(f32[4,1,512]{2,1,0:T(1,128)S(1)} %get-tuple-element.161), channel_id=1, source_target_pairs={{1,0},{2,1},{3,2},{4,3},{5,4},{6,5},{7,6},{8,7},{9,8},{10,9},{11,1... | collective-permute-start | bytes 24584 | tf_op jit(solution)/shard_map/ppermute | solution.py:22
  815.3 11.2 collective-permute-start.24
  818.5 4.4 collective-permute-start.21
  819.7 6.8 collective-permute-start.22
  959.6 13.7 %collective-permute-start.27 = (f32[4,1,512]{2,1,0:T(1,128)S(1)}, f32[4,1,512]{2,1,0:T(1,128)S(1)}, u32[]{:S(2)}, u32[]{:S(2)}) collective-permute-start(f32[4,1,512]{2,1,0:T(1,128)S(1)} %get-tuple-element.157), channel_id=1, source_target_pairs={{1,0},{2,1},{3,2},{4,3},{5,4},{6,5},{7,6},{8,7},{9,8},{10,9},{11,1... | collective-permute-start | bytes 24584 | tf_op jit(solution)/shard_map/ppermute | solution.py:22
  962.1 11.2 collective-permute-start.28
  965.3 4.4 collective-permute-start.25
  966.4 6.8 collective-permute-start.26
  1108.0 13.7 %collective-permute-start.31 = (f32[4,1,512]{2,1,0:T(1,128)S(1)}, f32[4,1,512]{2,1,0:T(1,128)S(1)}, u32[]{:S(2)}, u32[]{:S(2)}) collective-permute-start(f32[4,1,512]{2,1,0:T(1,128)S(1)} %get-tuple-element.153), channel_id=1, source_target_pairs={{1,0},{2,1},{3,2},{4,3},{5,4},{6,5},{7,6},{8,7},{9,8},{10,9},{11,1... | collective-permute-start | bytes 24584 | tf_op jit(solution)/shard_map/ppermute | solution.py:22
  1110.5 11.2 collective-permute-start.32
  1113.7 4.4 collective-permute-start.29
  1114.9 6.8 collective-permute-start.30
  1257.8 13.7 %collective-permute-start.35 = (f32[4,1,512]{2,1,0:T(1,128)S(1)}, f32[4,1,512]{2,1,0:T(1,128)S(1)}, u32[]{:S(2)}, u32[]{:S(2)}) collective-permute-start(f32[4,1,512]{2,1,0:T(1,128)S(1)} %get-tuple-element.149), channel_id=1, source_target_pairs={{1,0},{2,1},{3,2},{4,3},{5,4},{6,5},{7,6},{8,7},{9,8},{10,9},{11,1... | collective-permute-start | bytes 24584 | tf_op jit(solution)/shard_map/ppermute | solution.py:22
  1260.2 11.2 collective-permute-start.36
  1263.4 4.4 collective-permute-start.33
  1264.6 6.8 collective-permute-start.34
  (2 other events, 43.2 us)
where the time goes:
time: 1350 us; the launch traced here: 1340 us
  blocking collectives  973 us (72%)
  waiting for transfers between devices  128 us (9%)
  local copies, waits for them, and re-layouts  118 us (9%)
  starting transfers between devices  78.1 us (6%)
  other arithmetic  23.4 us (2%)
  between operations  20.7 us (2%)
    psum x8, blocking collectives, squares(): return lax.psum(jnp.sum(residual * residual), ('lon', 'lat'))  510 us
    psum x7, blocking collectives, body(): lax.psum(jnp.sum(direction * applied), ('lon', 'lat'))  464 us
    ppermute x7, waiting for transfers between devices, shifted(): return lax.ppermute(x, axis, [(i, (i + by) % peers) for i in range(peers)])  78.7 us
    ppermute x18, starting transfers between devices, with_halo(): lax.ppermute(head, axis, [((i + 1) % count, i) for i in range(ends)])  45 us
    slice x1, local copies, waits for them, and re-layouts, band_row(): summed = weights[0] * window[:, 0:length]  33.2 us
    unnamed x20, local copies, waits for them, and re-layouts  32 us
    ppermute x18, starting transfers between devices, with_halo(): lax.ppermute(tail, axis, [(i, (i + 1) % count) for i in range(ends)])  31.3 us
    ppermute x18, waiting for transfers between devices, with_halo(): lax.ppermute(tail, axis, [(i, (i + 1) % count) for i in range(ends)])  30.3 us
  transfers between devices with their start and end apart: 43, of which 24 were waited for; matrix products, arithmetic and copies ran while one was open for 0% of the time, Pallas kernels for 0%

commit v1 on v0

--- a/solution.py
+++ b/solution.py
@@ -3,6 +3,8 @@
 import jax
 import jax.numpy as jnp
 from jax import lax
+from jax.experimental import pallas as pl
+from jax.experimental.pallas import tpu as pltpu
 from jax.sharding import PartitionSpec as P
 
 DRIFT = 8
@@ -67,6 +69,403 @@
     return lax.psum(jnp.sum(residual * residual), ("lon", "lat"))
 
 
+MESH = pl.DeviceIdType.MESH
+F32 = jnp.float32
+STEPS = 4
+LOW, REST = 0.05, 9.0
+LIMIT = 1.5e4
+ROWS, COLS = 48, 512
+XR, XC = 56, 640
+
+
+def iota(shape, dim):
+    return lax.broadcasted_iota(jnp.int32, shape, dim)
+
+
+class Remote:
+    def __init__(self, send_sems, recv_sems):
+        self.send_sems, self.recv_sems, self.used, self.all = send_sems, recv_sems, 0, []
+
+    def start(self, src, dst, lon, lat):
+        copy = pltpu.make_async_remote_copy(
+            src_ref=src,
+            dst_ref=dst,
+            send_sem=self.send_sems.at[self.used],
+            recv_sem=self.recv_sems.at[self.used],
+            device_id=(lon, lat),
+            device_id_type=MESH,
+        )
+        self.used += 1
+        copy.start()
+        self.all.append(copy)
+        return copy
+
+    def drain(self):
+        for copy in self.all:
+            copy.wait_send()
+
+
+def coefficients(gram, steps, middle, half, final):
+    shared = gram.shared
+    base = 0 if shared else steps + 1
+
+    def apply(vec):
+        out = {}
+
+        def add(i, x):
+            out[i] = out[i] + x if i in out else x
+
+        for i, x in vec.items():
+            start = 0 if i <= steps else steps + 1
+            add(i, x * middle)
+            if i == start:
+                add(i + 1, x * half)
+            else:
+                add(i + 1, x * (0.5 * half))
+                add(i - 1, x * (0.5 * half))
+        return out
+
+    def form(a, b):
+        total = size = None
+        for i, x in a.items():
+            inner = bulk = None
+            for j, y in b.items():
+                term = gram(i, j) * y
+                inner = term if inner is None else inner + term
+                bulk = jnp.abs(term) if bulk is None else bulk + jnp.abs(term)
+            total = x * inner if total is None else total + x * inner
+            size = jnp.abs(x) * bulk if size is None else size + jnp.abs(x) * bulk
+        return total, size / jnp.abs(total)
+
+    def plus(a, scale, b):
+        return {i: a[i] + scale * b[i] if i in a and i in b else (a[i] if i in a else scale * b[i]) for i in {**a, **b}}
+
+    one = jnp.ones((8, 128), F32)
+    direction, residual, answer = {0: one}, {base: one}, {}
+    norm, worst = gram(base, base), one
+    for count in range(steps):
+        applied = apply(direction)
+        slope, size = form(direction, applied)
+        worst = jnp.maximum(worst, size)
+        rate = norm / slope
+        answer = plus(answer, rate, direction)
+        if not (final and count == steps - 1):
+            residual = plus(residual, -rate, applied)
+            follow, size = form(residual, residual)
+            worst = jnp.maximum(worst, size)
+            direction = plus(residual, follow / norm, direction)
+            norm = follow
+    return answer, direction, residual, worst
+
+
+class Gram:
+    def __init__(self, row, pairs, shared):
+        self.row, self.place, self.shared, self.cache = row, {p: i for i, p in enumerate(pairs)}, shared, {}
+
+    def __call__(self, i, j):
+        pair = (min(i, j), max(i, j))
+        if pair not in self.cache:
+            at = self.place[pair]
+            self.cache[pair] = jnp.broadcast_to(self.row[:, at : at + 1], (8, 128))
+        return self.cache[pair]
+
+
+def solve_kernel(
+    nlon, nlat, vertical, dep, helm, out, flag,
+    vs, dd, lat_in, lon_in, packs, stage, slot_lon, slot_lat, local_sems, send_sems, recv_sems,
+):
+    lon, lat = lax.axis_index("lon"), lax.axis_index("lat")
+
+    def east(k):
+        return lax.rem(lon + (k + nlon), nlon)
+
+    def north(k):
+        return lax.rem(lat + (k + nlat), nlat)
+
+    own = [
+        pltpu.make_async_copy(helm, dd.at[:, pl.ds(0, ROWS), pl.ds(0, COLS)], local_sems.at[0]),
+        pltpu.make_async_copy(dep, vs.at[0, pl.ds(1, 4), pl.ds(0, ROWS), pl.ds(0, COLS)], local_sems.at[1]),
+    ]
+    for copy in own:
+        copy.start()
+    barrier = pltpu.get_barrier_semaphore()
+    greeted = 0
+    for k in range(1, nlon):
+        pl.semaphore_signal(barrier, inc=1, device_id=(east(k), lat), device_id_type=MESH)
+        greeted += 1
+    for k in range(1, nlat):
+        pl.semaphore_signal(barrier, inc=1, device_id=(lon, north(k)), device_id_type=MESH)
+        greeted += 1
+    for a in (-1, 1):
+        for b in (-1, 1):
+            pl.semaphore_signal(barrier, inc=1, device_id=(east(a), north(b)), device_id_type=MESH)
+            greeted += 1
+
+    remote = Remote(send_sems, recv_sems)
+    lane, sub = iota((8, 128), 1), iota((8, 128), 0)
+    top_ok, bottom_ok = lat > 0, lat < nlat - 1
+
+    zero = jnp.zeros((XR, XC), F32)
+    for j in range(2 * STEPS + 1):
+        vs[j, 0] = zero
+        vs[j, 5] = zero
+    stage[...] = jnp.zeros_like(stage)
+
+    biggest = jnp.maximum(jnp.maximum(vertical[0], vertical[1]), jnp.maximum(vertical[2], vertical[3]))
+    top = REST + 4.0 * biggest
+    middle, half = 0.5 * (top + LOW), 0.5 * (top - LOW)
+    double = (jnp.full((8, 128), 2.0, F32) / jnp.broadcast_to(half, (8, 128)))
+
+    def start_exchange(tile, rows, which):
+        right = left = jnp.zeros((8, 128), F32)
+        for i in range(24):
+            here = lane // 4 == i
+            right = jnp.where(here, pltpu.roll(tile(i // 6, i % 6, 3), (4 * i + 4) % 128, 1), right)
+            left = jnp.where(here, pltpu.roll(tile(i // 6, i % 6, 0), (4 * i) % 128, 1), left)
+        packs[which, 0] = right
+        packs[which, 1] = left
+        return [
+            remote.start(rows(40), lat_in.at[which, 0], lon, north(1)),
+            remote.start(rows(0), lat_in.at[which, 1], lon, north(-1)),
+            remote.start(packs.at[which, 0], lon_in.at[which, 0], east(1), lat),
+            remote.start(packs.at[which, 0], lon_in.at[which, 1], east(1), north(1)),
+            remote.start(packs.at[which, 0], lon_in.at[which, 2], east(1), north(-1)),
+            remote.start(packs.at[which, 1], lon_in.at[which, 3], east(-1), lat),
+            remote.start(packs.at[which, 1], lon_in.at[which, 4], east(-1), north(1)),
+            remote.start(packs.at[which, 1], lon_in.at[which, 5], east(-1), north(-1)),
+        ]
+
+    def finish_exchange(copies, put, which):
+        for copy in copies:
+            copy.wait_recv()
+        ok = jnp.where(sub < 4, bottom_ok.astype(jnp.int32), top_ok.astype(jnp.int32)) > 0
+        packed = [lon_in[which, i] for i in range(6)]
+        for level in range(4):
+            for t in range(7):
+                if t < 6:
+                    i = level * 6 + t
+                    west, east_ = packed[0], packed[3]
+                    westward = pltpu.roll(west, (124 - 4 * i) % 128, 1)
+                    eastward = pltpu.roll(east_, (-4 * i) % 128, 1)
+                    put(level, t, 4, jnp.where(lane < 64, eastward, westward))
+                else:
+                    first, last = level * 6, level * 6 + 5
+                    westward = jnp.where(
+                        sub < 4,
+                        pltpu.roll(packed[2], (124 - 4 * first) % 128, 1),
+                        pltpu.roll(packed[1], (124 - 4 * last) % 128, 1),
+                    )
+                    eastward = jnp.where(
+                        sub < 4,
+                        pltpu.roll(packed[5], (-4 * first) % 128, 1),
+                        pltpu.roll(packed[4], (-4 * last) % 128, 1),
+                    )
+                    put(level, t, 4, jnp.where(ok, jnp.where(lane < 64, eastward, westward), 0.0))
+            for b in range(4):
+                above = lat_in[which, 0, level, :, 128 * b : 128 * b + 128]
+                below = lat_in[which, 1, level, :, 128 * b : 128 * b + 128]
+                put(level, 6, b, jnp.where(ok, jnp.where(sub < 4, below, above), 0.0))
+
+    def vector(j):
+        def tile(level, t, b):
+            return vs[j, level + 1, 8 * t : 8 * t + 8, 128 * b : 128 * b + 128]
+
+        def put(level, t, b, value):
+            vs[j, level + 1, 8 * t : 8 * t + 8, 128 * b : 128 * b + 128] = value
+
+        def rows(at):
+            return vs.at[j, pl.ds(1, 4), pl.ds(at, 8), pl.ds(0, COLS)]
+
+        return tile, rows, put
+
+    def diag_tile(level, t, b):
+        return dd[level, 8 * t : 8 * t + 8, 128 * b : 128 * b + 128]
+
+    def diag_put(level, t, b, value):
+        dd[level, 8 * t : 8 * t + 8, 128 * b : 128 * b + 128] = value
+
+    def diag_rows(at):
+        return dd.at[:, pl.ds(at, 8), pl.ds(0, COLS)]
+
+    def wide(x, shape):
+        return jnp.broadcast_to(x[0:1, 0:1], shape)
+
+    def chebyshev(src, before, dst):
+        mask = jnp.where(iota((8, XC), 0) < 4, bottom_ok.astype(F32), top_ok.astype(F32))
+        scale = wide(double, (XR, XC))
+
+        def one(level, carry):
+            mid = vs[src, level + 1]
+            sides = pltpu.roll(mid, 1, 1) + pltpu.roll(mid, XC - 1, 1)
+            sides = sides + (pltpu.roll(mid, 1, 0) + pltpu.roll(mid, XR - 1, 0))
+            stack = vs[src, level] + vs[src, level + 2]
+            value = dd[level] * mid - scale * (sides + vertical[level] * stack)
+            value = 0.5 * value if before is None else value - vs[before, level + 1]
+            vs[dst, level + 1, 0:ROWS, :] = value[0:ROWS]
+            vs[dst, level + 1, ROWS:XR, :] = value[ROWS:XR] * mask
+            return carry
+
+        lax.fori_loop(0, 4, one, 0)
+
+    def build(base, count):
+        for k in range(1, count):
+            chebyshev(base + k - 1, None if k == 1 else base + k - 2, base + k)
+
+    def all_reduce(value, turn):
+        slot_lon[turn, lon] = value
+        copies = [
+            remote.start(slot_lon.at[turn, lon], slot_lon.at[turn, lon], east(k), lat) for k in range(1, nlon)
+        ]
+        for copy in copies:
+            copy.wait_recv()
+        value = slot_lon[turn, 0]
+        for i in range(1, nlon):
+            value = value + slot_lon[turn, i]
+        slot_lat[turn, lat] = value
+        copies = [
+            remote.start(slot_lat.at[turn, lat], slot_lat.at[turn, lat], lon, north(k)) for k in range(1, nlat)
+        ]
+        for copy in copies:
+            copy.wait_recv()
+        value = slot_lat[turn, 0]
+        for i in range(1, nlat):
+            value = value + slot_lat[turn, i]
+        return value
+
+    def gram(count, turn, shared):
+        pairs = [(i, j) for i in range(count) for j in range(i, count)]
+
+        def one(t, sums):
+            level, r = t // 6, pl.multiple_of((t % 6) * 8, 8)
+            sums = list(sums)
+            for b in range(4):
+                tiles = [vs[i, level + 1, pl.ds(r, 8), 128 * b : 128 * b + 128] for i in range(count)]
+                for n, (i, j) in enumerate(pairs):
+                    sums[n] = sums[n] + tiles[i] * tiles[j]
+            return tuple(sums)
+
+        sums = lax.fori_loop(0, 24, one, tuple(jnp.zeros((8, 128), F32) for _ in pairs))
+        for n, part in enumerate(sums):
+            stage[n : n + 1, :] = jnp.sum(part, axis=0, keepdims=True)
+        row = lax.dot_general(
+            jnp.ones((8, 128), F32), stage[...], (((1,), (1,)), ((), ())),
+            precision=lax.Precision.HIGHEST, preferred_element_type=F32,
+        )
+        return Gram(all_reduce(row, turn), pairs, shared)
+
+    def combine(count, outputs):
+        def one(t, carry):
+            level, r = t // 6, pl.multiple_of((t % 6) * 8, 8)
+            for b in range(4):
+                tiles = [vs[i, level + 1, pl.ds(r, 8), 128 * b : 128 * b + 128] for i in range(count)]
+                values = []
+                for coef, _ in outputs:
+                    value = None
+                    for i, x in coef.items():
+                        value = x * tiles[i] if value is None else value + x * tiles[i]
+                    values.append(value)
+                for value, (_, write) in zip(values, outputs):
+                    write(level, pl.ds(r, 8), pl.ds(128 * b, 128), value)
+            return carry
+
+        lax.fori_loop(0, 24, one, 0)
+
+    def put_out(level, r, b, value):
+        out[level, r, b] = value
+
+    def add_out(level, r, b, value):
+        out[level, r, b] = out[level, r, b] + value
+
+    def put_vector(j):
+        def write(level, r, b, value):
+            vs[j, level + 1, r, b] = value
+
+        return write
+
+    for copy in own:
+        copy.wait()
+    pl.semaphore_wait(barrier, greeted)
+
+    b_tile, b_rows, b_put = vector(0)
+    waiting = [start_exchange(diag_tile, diag_rows, 0), start_exchange(b_tile, b_rows, 1)]
+    finish_exchange(waiting[0], diag_put, 0)
+
+    def shift_diag(level, carry):
+        add = 4.0 + 2.0 * vertical[level] - middle
+        dd[level] = wide(double, (XR, XC)) * (dd[level] + add)
+        return carry
+
+    remote.drain()
+    remote.all.clear()
+    lax.fori_loop(0, 4, shift_diag, 0)
+    finish_exchange(waiting[1], b_put, 1)
+    build(0, STEPS + 1)
+    answer, direction, residual, worst = coefficients(gram(STEPS + 1, 0, True), STEPS, middle, half, False)
+    combine(
+        STEPS + 1,
+        [(answer, put_out), (direction, put_vector(0)), (residual, put_vector(STEPS + 1))],
+    )
+    p_tile, p_rows, p_put = vector(0)
+    r_tile, r_rows, r_put = vector(STEPS + 1)
+    waiting = [start_exchange(p_tile, p_rows, 2), start_exchange(r_tile, r_rows, 3)]
+    finish_exchange(waiting[0], p_put, 2)
+    build(0, STEPS + 1)
+    finish_exchange(waiting[1], r_put, 3)
+    build(STEPS + 1, STEPS)
+    answer, _, _, second = coefficients(gram(2 * STEPS + 1, 1, False), STEPS, middle, half, True)
+    combine(2 * STEPS + 1, [(answer, add_out)])
+    flag[...] = jnp.maximum(worst, second)
+    remote.drain()
+
+
+def solve(departure, helm_diag, vertical, nlon, nlat):
+    copies = 4 * 8 + 2 * (nlon - 1 + nlat - 1)
+    vmem = pl.BlockSpec(memory_space=pltpu.VMEM)
+    anywhere = pl.BlockSpec(memory_space=pl.ANY)
+    return pl.pallas_call(
+        partial(solve_kernel, nlon, nlat),
+        out_shape=(
+            jax.ShapeDtypeStruct(departure.shape, F32),
+            jax.ShapeDtypeStruct((8, 128), F32),
+        ),
+        in_specs=[pl.BlockSpec(memory_space=pltpu.SMEM), anywhere, anywhere],
+        out_specs=(vmem, vmem),
+        scratch_shapes=[
+            pltpu.VMEM((2 * STEPS + 1, 6, XR, XC), F32),
+            pltpu.VMEM((4, XR, XC), F32),
+            pltpu.VMEM((4, 2, 4, 8, COLS), F32),
+            pltpu.VMEM((4, 6, 8, 128), F32),
+            pltpu.VMEM((4, 2, 8, 128), F32),
+            pltpu.VMEM((128, 128), F32),
+            pltpu.VMEM((2, nlon, 8, 128), F32),
+            pltpu.VMEM((2, nlat, 8, 128), F32),
+            pltpu.SemaphoreType.DMA((2,)),
+            pltpu.SemaphoreType.DMA((copies,)),
+            pltpu.SemaphoreType.DMA((copies,)),
+        ],
+        compiler_params=pltpu.CompilerParams(
+            collective_id=0, has_side_effects=True, vmem_limit_bytes=40 * 1024 * 1024
+        ),
+        name="solve",
+    )(vertical, departure, helm_diag)
+
+
+def iterate(departure, helm_diag, vertical):
+    def one(_, carry):
+        answer, residual, direction, norm = carry
+        applied = operate(direction, helm_diag, vertical)
+        rate = norm / lax.psum(jnp.sum(direction * applied), ("lon", "lat"))
+        answer = answer + rate * direction
+        residual = residual - rate * applied
+        follow = squares(residual)
+        return answer, residual, residual + follow / norm * direction, follow
+
+    start = (jnp.zeros_like(departure), departure, departure, squares(departure))
+    answer, _, direction, norm = lax.fori_loop(0, ITERS - 1, one, start)
+    applied = operate(direction, helm_diag, vertical)
+    return answer + norm / lax.psum(jnp.sum(direction * applied), ("lon", "lat")) * direction
+
+
 def body(source_field, helm_diag, vertical, cubic_band, lat_offset, zonal_shift, row_class):
     levels, lat_rows, lon_cells = source_field.shape
     lon_count = lax.axis_size("lon")
@@ -92,20 +491,11 @@
     moved = lax.fori_loop(1, lon_count, advance, (picked, picked))[1]
     framed = with_halo(moved, (("lon", 2),), lon_cells, True)
     departure = finish(framed, remain, row_table, lon_cells)
-    solution = jnp.zeros_like(departure)
-    residual = departure
-    direction = departure
-    norm_now = squares(residual)
-    for iteration in range(ITERS):
-        applied = operate(direction, helm_diag, vertical)
-        step_size = norm_now / lax.psum(jnp.sum(direction * applied), ("lon", "lat"))
-        solution = solution + step_size * direction
-        if iteration + 1 < ITERS:
-            residual = residual - step_size * applied
-            norm_next = squares(residual)
-            direction = residual + norm_next / norm_now * direction
-            norm_now = norm_next
-    return (departure, solution)
+    quick, worst = solve(departure, helm_diag, vertical, lon_count, lax.axis_size("lat"))
+    answer = lax.cond(
+        worst[0, 0] < LIMIT, lambda *_: quick, iterate, departure, helm_diag, vertical
+    )
+    return (departure, answer)
 
 
 def solution(mesh):

time: 1350 us -> 283 us (0.21)
  blocking collectives: 973 us -> 0 us
  Pallas kernels: 0 us -> 66.9 us
  starting transfers between devices: 78.1 us -> 11.9 us
  waiting for transfers between devices: 128 us -> 79.9 us
  other arithmetic: 23.4 us -> 3.65 us
  between operations: 20.7 us -> 1.49 us
    psum x15 -> x0, blocking collectives: 973 us -> none  [the longest x8 510 us: squares(): return lax.psum(jnp.sum(residual * residual), ('lon', 'lat'))]
    pallas_call x0 -> x1, Pallas kernels: none -> 66.9 us  [solve(): pl.pallas_call(partial(solve_kernel, nlon, nlat), out_shape=(jax.ShapeDty...]
    ppermute x18 -> x2, starting transfers between devices: 45 us -> 6.89 us  [with_halo(): lax.ppermute(head, axis, [((i + 1) % count, i) for i in range(ends)])]
    ppermute x18 -> x2, starting transfers between devices: 31.3 us -> 3.26 us  [with_halo(): lax.ppermute(tail, axis, [(i, (i + 1) % count) for i in range(ends)])]
    ppermute x18 -> x2, waiting for transfers between devices: 30.3 us -> 5.63 us  [with_halo(): lax.ppermute(tail, axis, [(i, (i + 1) % count) for i in range(ends)])]
    ppermute x18 -> x2, waiting for transfers between devices: 19.3 us -> 0.01 us  [with_halo(): lax.ppermute(head, axis, [((i + 1) % count, i) for i in range(ends)])]
    reduce_sum x15 -> x0, other arithmetic: 16.9 us -> none  [the longest x8 9.69 us: body(): jnp.sum(direction * applied)]
    unnamed x20 -> x17, local copies, waits for them, and re-layouts: 32 us -> 32.7 us
  transfers between devices with their start and end apart: 43 -> 11, of which waited for: 24 -> 8; matrix products, arithmetic and copies ran while one was open for 0% -> 1% of each run, Pallas kernels for 0% -> 0%
where the time goes in v1:
time: 283 us
  local copies, waits for them, and re-layouts  118 us (42%)
  waiting for transfers between devices  79.9 us (28%)
  Pallas kernels  66.9 us (24%)
  starting transfers between devices  11.9 us (4%)
  other arithmetic  3.65 us (1%)
    ppermute x7, waiting for transfers between devices, shifted(): return lax.ppermute(x, axis, [(i, (i + by) % peers) for i in range(peers)])  74.3 us
    pallas_call x1, Pallas kernels, solve(): pl.pallas_call(partial(solve_kernel, nlon, nlat), out_shape=(jax.ShapeDty...  66.9 us
    slice x1, local copies, waits for them, and re-layouts, band_row(): summed = weights[0] * window[:, 0:length]  33.2 us
    unnamed x17, local copies, waits for them, and re-layouts  32.7 us
    gather x1, local copies, waits for them, and re-layouts, band_row(): window = lax.dynamic_slice_in_dim(row_cells, begin_at, length + 3, 1)  27.2 us
    concatenate x1, local copies, waits for them, and re-layouts, with_halo(): jnp.concatenate([lax.ppermute(tail, axis, [(i, (i + 1) % count) for i in...  23.6 us
    ppermute x2, starting transfers between devices, with_halo(): lax.ppermute(head, axis, [((i + 1) % count, i) for i in range(ends)])  6.89 us
  transfers between devices with their start and end apart: 11, of which 8 were waited for; matrix products, arithmetic and copies ran while one was open for 1% of the time, Pallas kernels for 0%

profile of v1, /device:TPU:1, one launch (start us, length us, event | category | flops | bytes accessed | tf_op | source)
XLA Modules:
  0.0 282.7 jit_solution(8768160615719160751)
XLA Ops:
  0.6 0.0 copy-start
  0.7 1.3 copy.28
  1.9 3.3 %collective-permute-start.10 = (f32[4,8,512]{2,0,1:T(4,128)S(1)}, f32[4,8,512]{2,0,1:T(4,128)S(1)}, u32[]{:S(2)}, u32[]{:S(2)}) collective-permute-start(f32[4,8,512]{2,0,1:T(4,128)S(1)} %get-tuple-element.267), channel_id=1, source_target_pairs={{1,0},{2,1},{3,2},{4,3},{5,4},{6,5},{7,6},{8,7},{9,8},{10,9},{11,1... | collective-permute-start | bytes 196616 | tf_op jit(solution)/shard_map/ppermute | solution.py:24
  5.3 3.2 %collective-permute-start.9 = (f32[4,8,512]{2,0,1:T(4,128)S(1)}, f32[4,8,512]{2,0,1:T(4,128)S(1)}, u32[]{:S(2)}, u32[]{:S(2)}) collective-permute-start(f32[4,8,512]{2,0,1:T(4,128)S(1)} %get-tuple-element.266), channel_id=1, source_target_pairs={{0,1},{1,2},{2,3},{3,4},{4,5},{5,6},{6,7},{7,8},{8,9},{9,10},{10,1... | collective-permute-start | bytes 196616 | tf_op jit(solution)/shard_map/ppermute | solution.py:22
  8.5 0.7 compare_and_fusion
  9.1 0.7 fusion.21
  9.9 0.1 pad_maximum_fusion.9
  10.0 0.8 gather_fusion
  10.8 0.2 select_bitcast_fusion
  10.9 0.1 copy.31
  11.1 77.4 %while.34 = (s32[]{:T(128)}, f32[4,48,512]{2,1,0:T(8,128)S(1)}, f32[4,48,512]{2,1,0:T(8,128)S(1)}, s32[1,48,1]{1,2,0:T(1,128)S(1)}, s32[]{:T(128)}) while((s32[]{:T(128)}, f32[4,48,512]{2,1,0:T(8,128)S(1)}, f32[4,48,512]{2,1,0:T(8,128)S(1)}, s32[1,48,1]{1,2,0:T(1,128)S(1)}, s32[]{:T(128)}) %tuple.94), condition=%wide.region_1.2_spmd, body=%wide.region_0.1_spmd.sunk | while | flops 98354 | bytes 3539337 | solution.py:491
  11.1 1.3 collective-permute-start
  12.4 12.2 %collective-permute-done = f32[4,48,512]{2,1,0:T(8,128)S(1)} collective-permute-done((f32[4,48,512]{2,1,0:T(8,128)S(1)}, f32[4,48,512]{2,1,0:T(8,128)S(1)}, u32[]{:S(2)}, u32[]{:S(2)}) %collective-permute-start) | collective-permute-done | bytes 393248 | tf_op jit(solution)/shard_map/while/body/eval_jaxpr/ppermute | solution.py:33
  24.6 0.1 broadcast_select_fusion.2
  24.8 0.1 collective-permute-start
  24.9 12.5 %collective-permute-done = f32[4,48,512]{2,1,0:T(8,128)S(1)} collective-permute-done((f32[4,48,512]{2,1,0:T(8,128)S(1)}, f32[4,48,512]{2,1,0:T(8,128)S(1)}, u32[]{:S(2)}, u32[]{:S(2)}) %collective-permute-start) | collective-permute-done | bytes 393248 | tf_op jit(solution)/shard_map/while/body/eval_jaxpr/ppermute | solution.py:33
  37.5 0.1 broadcast_select_fusion.2
  37.6 0.1 collective-permute-start
  37.7 11.6 %collective-permute-done = f32[4,48,512]{2,1,0:T(8,128)S(1)} collective-permute-done((f32[4,48,512]{2,1,0:T(8,128)S(1)}, f32[4,48,512]{2,1,0:T(8,128)S(1)}, u32[]{:S(2)}, u32[]{:S(2)}) %collective-permute-start) | collective-permute-done | bytes 393248 | tf_op jit(solution)/shard_map/while/body/eval_jaxpr/ppermute | solution.py:33
  49.4 0.1 broadcast_select_fusion.2
  49.5 0.1 collective-permute-start
  49.6 10.7 %collective-permute-done = f32[4,48,512]{2,1,0:T(8,128)S(1)} collective-permute-done((f32[4,48,512]{2,1,0:T(8,128)S(1)}, f32[4,48,512]{2,1,0:T(8,128)S(1)}, u32[]{:S(2)}, u32[]{:S(2)}) %collective-permute-start) | collective-permute-done | bytes 393248 | tf_op jit(solution)/shard_map/while/body/eval_jaxpr/ppermute | solution.py:33
  60.3 0.1 broadcast_select_fusion.2
  60.5 0.1 collective-permute-start
  60.6 9.8 %collective-permute-done = f32[4,48,512]{2,1,0:T(8,128)S(1)} collective-permute-done((f32[4,48,512]{2,1,0:T(8,128)S(1)}, f32[4,48,512]{2,1,0:T(8,128)S(1)}, u32[]{:S(2)}, u32[]{:S(2)}) %collective-permute-start) | collective-permute-done | bytes 393248 | tf_op jit(solution)/shard_map/while/body/eval_jaxpr/ppermute | solution.py:33
  70.4 0.1 broadcast_select_fusion.2
  70.6 0.1 collective-permute-start
  70.7 8.7 %collective-permute-done = f32[4,48,512]{2,1,0:T(8,128)S(1)} collective-permute-done((f32[4,48,512]{2,1,0:T(8,128)S(1)}, f32[4,48,512]{2,1,0:T(8,128)S(1)}, u32[]{:S(2)}, u32[]{:S(2)}) %collective-permute-start) | collective-permute-done | bytes 393248 | tf_op jit(solution)/shard_map/while/body/eval_jaxpr/ppermute | solution.py:33
  79.4 0.1 broadcast_select_fusion.2
  79.6 0.1 collective-permute-start
  79.6 8.7 %collective-permute-done = f32[4,48,512]{2,1,0:T(8,128)S(1)} collective-permute-done((f32[4,48,512]{2,1,0:T(8,128)S(1)}, f32[4,48,512]{2,1,0:T(8,128)S(1)}, u32[]{:S(2)}, u32[]{:S(2)}) %collective-permute-start) | collective-permute-done | bytes 393248 | tf_op jit(solution)/shard_map/while/body/eval_jaxpr/ppermute | solution.py:33
  88.4 0.1 broadcast_select_fusion.2
  88.5 0.1 collective-permute-start.11
  88.6 3.6 %collective-permute-start.12 = (f32[4,48,512]{2,1,0:T(8,128)S(1)}, f32[4,48,512]{2,1,0:T(8,128)S(1)}, u32[]{:S(2)}, u32[]{:S(2)}) collective-permute-start(f32[4,48,512]{2,1,0:T(8,128)S(1)} %get-tuple-element.187), channel_id=1, source_target_pairs={{16,0},{32,16},{48,32},{64,48},{80,64},{96,80},{112,96},{0,112},{1... | collective-permute-start | bytes 1179656 | tf_op jit(solution)/shard_map/ppermute | solution.py:24
  92.2 0.2 fusion.16
  92.4 5.6 %collective-permute-done.11 = f32[4,48,512]{2,1,0:T(8,128)S(1)} collective-permute-done((f32[4,48,512]{2,1,0:T(8,128)S(1)}, f32[4,48,512]{2,1,0:T(8,128)S(1)}, u32[]{:S(2)}, u32[]{:S(2)}) %collective-permute-start.11) | collective-permute-done | bytes 393248 | tf_op jit(solution)/shard_map/ppermute | solution.py:22
  98.0 0.1 pad_maximum_fusion.8
  98.1 23.6 %copy.33 = f32[4,48,1536]{0,1,2:T(8,128)} copy(f32[4,48,1536]{2,1,0:T(8,128)S(1)} %pad_maximum_fusion.8) | data formatting | bytes 2359296 | tf_op jit(solution)/shard_map/concatenate | solution.py:20
  121.7 27.2 %gather_fusion.1 = f32[48,4,515]{1,0,2:T(8,128)} fusion(f32[48,4,1536]{1,0,2:T(8,128)} %bitcast.27, s32[48]{0:T(128)S(1)} %get-tuple-element.248), kind=kCustom, calls=%fused_computation.1 | custom fusion | bytes 791616 | tf_op jit(solution)/shard_map/vmap()/gather | solution.py:37
  149.0 33.2 %fusion.28 = (f32[48,4,512]{1,0,2:T(8,128)}, f32[48,4,512]{1,0,2:T(8,128)}, f32[48,4,512]{1,0,2:T(8,128)}, f32[48,4,512]{1,0,2:T(8,128)}) fusion(f32[48,4,515]{1,0,2:T(8,128)} %gather_fusion.1), kind=kLoop, calls=%fused_computation.74 | loop fusion | bytes 3145728 | tf_op jit(solution)/shard_map/vmap()/slice | solution.py:38
  182.2 7.6 %copy.38 = f32[48,4,512]{2,0,1:T(8,128)S(1)} copy(f32[48,4,512]{1,0,2:T(8,128)} %get-tuple-element.262) | data formatting | bytes 786432
  189.8 7.7 %copy.39 = f32[48,4,512]{2,0,1:T(8,128)S(1)} copy(f32[48,4,512]{1,0,2:T(8,128)} %get-tuple-element.264) | data formatting | bytes 786432
  197.5 7.7 %copy.40 = f32[48,4,512]{2,0,1:T(8,128)S(1)} copy(f32[48,4,512]{1,0,2:T(8,128)} %get-tuple-element.263) | data formatting | bytes 786432
  205.2 7.6 %copy.41 = f32[48,4,512]{2,0,1:T(8,128)S(1)} copy(f32[48,4,512]{1,0,2:T(8,128)} %get-tuple-element.265) | data formatting | bytes 786432
  212.9 0.9 add_bitcast_fusion.dep
  213.8 66.9 %solve.1 = (f32[4,48,512]{2,1,0:T(8,128)S(1)}, f32[8,128]{1,0:T(8,128)S(1)}) custom-call(f32[4]{0:T(128)S(1)} %copy-done.3, f32[4,48,512]{2,1,0:T(8,128)} %add_bitcast_fusion.dep, f32[4,48,512]{2,1,0:T(8,128)S(1)} %copy-done.2), custom_call_target="tpu_custom_call" | custom-call | tf_op jit(solution)/shard_map/solve/pallas_call | solution.py:425
  280.8 0.5 slice.141
  282.0 0.7 copy.71
  (32 shorter events, 0.3 us)
Async XLA Ops:
  0.6 91.6 %copy-start = (f32[8,4]{0,1:T(4,128)S(1)}, f32[8,4]{0,1:T(4,128)}, u32[]{:S(2)}) copy-start(f32[8,4]{0,1:T(4,128)} %param.16) | copy-start | bytes 388
  0.6 91.5 %copy-start.4 = (s32[48]{0:T(128)S(1)}, s32[48]{0:T(128)}, u32[]{:S(2)}) copy-start(s32[48]{0:T(128)} %param.19) | copy-start | bytes 580
  1.9 7.9 %collective-permute-start.10 = (f32[4,8,512]{2,0,1:T(4,128)S(1)}, f32[4,8,512]{2,0,1:T(4,128)S(1)}, u32[]{:S(2)}, u32[]{:S(2)}) collective-permute-start(f32[4,8,512]{2,0,1:T(4,128)S(1)} %get-tuple-element.267), channel_id=1, source_target_pairs={{1,0},{2,1},{3,2},{4,3},{5,4},{6,5},{7,6},{8,7},{9,8},{10,9},{11,1... | collective-permute-start | bytes 196616 | tf_op jit(solution)/shard_map/ppermute | solution.py:24
  5.3 4.6 %collective-permute-start.9 = (f32[4,8,512]{2,0,1:T(4,128)S(1)}, f32[4,8,512]{2,0,1:T(4,128)S(1)}, u32[]{:S(2)}, u32[]{:S(2)}) collective-permute-start(f32[4,8,512]{2,0,1:T(4,128)S(1)} %get-tuple-element.266), channel_id=1, source_target_pairs={{0,1},{1,2},{2,3},{3,4},{4,5},{5,6},{6,7},{7,8},{8,9},{9,10},{10,1... | collective-permute-start | bytes 196616 | tf_op jit(solution)/shard_map/ppermute | solution.py:22
  11.1 13.5 %collective-permute-start = (f32[4,48,512]{2,1,0:T(8,128)S(1)}, f32[4,48,512]{2,1,0:T(8,128)S(1)}, u32[]{:S(2)}, u32[]{:S(2)}) collective-permute-start(f32[4,48,512]{2,1,0:T(8,128)S(1)} %get-tuple-element.393), channel_id=1, source_target_pairs={{0,16},{16,32},{32,48},{48,64},{64,80},{80,96},{96,112},{112,0},{1... | collective-permute-start | bytes 1179656 | tf_op jit(solution)/shard_map/while/body/eval_jaxpr/ppermute | solution.py:33
  24.8 12.6 %collective-permute-start = (f32[4,48,512]{2,1,0:T(8,128)S(1)}, f32[4,48,512]{2,1,0:T(8,128)S(1)}, u32[]{:S(2)}, u32[]{:S(2)}) collective-permute-start(f32[4,48,512]{2,1,0:T(8,128)S(1)} %get-tuple-element.393), channel_id=1, source_target_pairs={{0,16},{16,32},{32,48},{48,64},{64,80},{80,96},{96,112},{112,0},{1... | collective-permute-start | bytes 1179656 | tf_op jit(solution)/shard_map/while/body/eval_jaxpr/ppermute | solution.py:33
  37.6 11.7 %collective-permute-start = (f32[4,48,512]{2,1,0:T(8,128)S(1)}, f32[4,48,512]{2,1,0:T(8,128)S(1)}, u32[]{:S(2)}, u32[]{:S(2)}) collective-permute-start(f32[4,48,512]{2,1,0:T(8,128)S(1)} %get-tuple-element.393), channel_id=1, source_target_pairs={{0,16},{16,32},{32,48},{48,64},{64,80},{80,96},{96,112},{112,0},{1... | collective-permute-start | bytes 1179656 | tf_op jit(solution)/shard_map/while/body/eval_jaxpr/ppermute | solution.py:33
  49.5 10.8 %collective-permute-start = (f32[4,48,512]{2,1,0:T(8,128)S(1)}, f32[4,48,512]{2,1,0:T(8,128)S(1)}, u32[]{:S(2)}, u32[]{:S(2)}) collective-permute-start(f32[4,48,512]{2,1,0:T(8,128)S(1)} %get-tuple-element.393), channel_id=1, source_target_pairs={{0,16},{16,32},{32,48},{48,64},{64,80},{80,96},{96,112},{112,0},{1... | collective-permute-start | bytes 1179656 | tf_op jit(solution)/shard_map/while/body/eval_jaxpr/ppermute | solution.py:33
  60.5 9.9 %collective-permute-start = (f32[4,48,512]{2,1,0:T(8,128)S(1)}, f32[4,48,512]{2,1,0:T(8,128)S(1)}, u32[]{:S(2)}, u32[]{:S(2)}) collective-permute-start(f32[4,48,512]{2,1,0:T(8,128)S(1)} %get-tuple-element.393), channel_id=1, source_target_pairs={{0,16},{16,32},{32,48},{48,64},{64,80},{80,96},{96,112},{112,0},{1... | collective-permute-start | bytes 1179656 | tf_op jit(solution)/shard_map/while/body/eval_jaxpr/ppermute | solution.py:33
  70.6 8.8 %collective-permute-start = (f32[4,48,512]{2,1,0:T(8,128)S(1)}, f32[4,48,512]{2,1,0:T(8,128)S(1)}, u32[]{:S(2)}, u32[]{:S(2)}) collective-permute-start(f32[4,48,512]{2,1,0:T(8,128)S(1)} %get-tuple-element.393), channel_id=1, source_target_pairs={{0,16},{16,32},{32,48},{48,64},{64,80},{80,96},{96,112},{112,0},{1... | collective-permute-start | bytes 1179656 | tf_op jit(solution)/shard_map/while/body/eval_jaxpr/ppermute | solution.py:33
  79.6 8.8 %collective-permute-start = (f32[4,48,512]{2,1,0:T(8,128)S(1)}, f32[4,48,512]{2,1,0:T(8,128)S(1)}, u32[]{:S(2)}, u32[]{:S(2)}) collective-permute-start(f32[4,48,512]{2,1,0:T(8,128)S(1)} %get-tuple-element.393), channel_id=1, source_target_pairs={{0,16},{16,32},{32,48},{48,64},{64,80},{80,96},{96,112},{112,0},{1... | collective-permute-start | bytes 1179656 | tf_op jit(solution)/shard_map/while/body/eval_jaxpr/ppermute | solution.py:33
  88.5 9.5 %collective-permute-start.11 = (f32[4,48,512]{2,1,0:T(8,128)S(1)}, f32[4,48,512]{2,1,0:T(8,128)S(1)}, u32[]{:S(2)}, u32[]{:S(2)}) collective-permute-start(f32[4,48,512]{2,1,0:T(8,128)S(1)} %get-tuple-element.187), channel_id=1, source_target_pairs={{0,16},{16,32},{32,48},{48,64},{64,80},{80,96},{96,112},{112,0},{1... | collective-permute-start | bytes 1179656 | tf_op jit(solution)/shard_map/ppermute | solution.py:22
  88.6 9.4 %collective-permute-start.12 = (f32[4,48,512]{2,1,0:T(8,128)S(1)}, f32[4,48,512]{2,1,0:T(8,128)S(1)}, u32[]{:S(2)}, u32[]{:S(2)}) collective-permute-start(f32[4,48,512]{2,1,0:T(8,128)S(1)} %get-tuple-element.187), channel_id=1, source_target_pairs={{16,0},{32,16},{48,32},{64,48},{80,64},{96,80},{112,96},{0,112},{1... | collective-permute-start | bytes 1179656 | tf_op jit(solution)/shard_map/ppermute | solution.py:24
  197.5 16.3 %copy-start.2 = (f32[4,48,512]{2,1,0:T(8,128)S(1)}, f32[4,48,512]{2,1,0:T(8,128)}, u32[]{:S(2)}) copy-start(f32[4,48,512]{2,1,0:T(8,128)} %helm.1) | copy-start | bytes 1179652
  197.5 16.3 %copy-start.3 = (f32[4]{0:T(128)S(1)}, f32[4]{0:T(128)}, u32[]{:S(2)}) copy-start(f32[4]{0:T(128)} %vertical.1) | copy-start | bytes 52
  281.9 0.8 copy-start.1

commit v2 on v1

--- a/solution.py
+++ b/solution.py
@@ -28,26 +28,6 @@
     return cells
 
 
-def shifted(x, axis, by):
-    peers = lax.axis_size(axis)
-    return lax.ppermute(x, axis, [(i, (i + by) % peers) for i in range(peers)])
-
-
-def band_row(row_cells, begin_at, weights, length):
-    window = lax.dynamic_slice_in_dim(row_cells, begin_at, length + 3, 1)
-    summed = weights[0] * window[:, 0:length]
-    summed = summed + weights[1] * window[:, 1 : length + 1]
-    summed = summed + weights[2] * window[:, 2 : length + 2]
-    summed = summed + weights[3] * window[:, 3 : length + 3]
-    return summed
-
-
-def finish(framed, remain, row_table, lon_cells):
-    begins = lon_cells - 128 * remain - 1
-    banded = jax.vmap(partial(band_row, length=lon_cells), in_axes=(1, 0, 0), out_axes=1)
-    return banded(framed, begins, row_table)
-
-
 def local_terms(values, helm_diag, vertical, east_west, north_south):
     stacked = jnp.pad(values, ((1, 1), (0, 0), (0, 0)))
     up_down = stacked[2:] + stacked[:-2]
@@ -99,6 +79,11 @@
         copy.start()
         self.all.append(copy)
         return copy
+
+    def settle(self, copies):
+        for copy in copies:
+            copy.wait_send()
+            self.all = [other for other in self.all if other is not copy]
 
     def drain(self):
         for copy in self.all:
@@ -171,7 +156,8 @@
 
 
 def solve_kernel(
-    nlon, nlat, vertical, dep, helm, out, flag,
+    nlon, nlat, vertical, band, offsets, shifts, classes, source, helm, dep, out, flag,
+    inner, upper, lower, picked, gathered, circle, banded, returned,
     vs, dd, lat_in, lon_in, packs, stage, slot_lon, slot_lat, local_sems, send_sems, recv_sems,
 ):
     lon, lat = lax.axis_index("lon"), lax.axis_index("lat")
@@ -184,7 +170,17 @@
 
     own = [
         pltpu.make_async_copy(helm, dd.at[:, pl.ds(0, ROWS), pl.ds(0, COLS)], local_sems.at[0]),
-        pltpu.make_async_copy(dep, vs.at[0, pl.ds(1, 4), pl.ds(0, ROWS), pl.ds(0, COLS)], local_sems.at[1]),
+        *[
+            pltpu.make_async_copy(
+                source.at[:, pl.ds(start, size), pl.ds(128 * b, 128)],
+                into.at[:, b, pl.ds(at, size), :],
+                local_sems.at[1 + 4 * n + b],
+            )
+            for n, (into, start, at, size) in enumerate(
+                [(inner, 0, 0, ROWS), (upper, 0, DRIFT, 2 * DRIFT), (lower, ROWS - 2 * DRIFT, 0, 2 * DRIFT)]
+            )
+            for b in range(4)
+        ],
     ]
     for copy in own:
         copy.start()
@@ -382,25 +378,150 @@
 
         return write
 
-    for copy in own:
+    for copy in own[1:5]:
         copy.wait()
+
+    def pick(j, part, write):
+        from_, first, rows = [(inner, 0, ROWS), (upper, -DRIFT, 3 * DRIFT), (lower, ROWS - 2 * DRIFT, 3 * DRIFT)][part]
+        row = jnp.clip(j + offsets[j] - first, 0, rows - 1)
+        for level in range(4):
+            for b in range(4):
+                write(4 * level + b, from_[level, b, pl.ds(row, 1), :])
+
+    def pick_rows(c, k, rows, at, parts):
+        for n, (j, part) in enumerate(zip(rows, parts)):
+
+            def write(place, value, n=n):
+                if k == nlon:
+                    gathered[c, at + 16 * n + place : at + 16 * n + place + 1, :] = value
+                else:
+                    picked[k - 1, at + 16 * n + place : at + 16 * n + place + 1, :] = value
+
+            pick(j, part, write)
+
+    def middle_rows(c):
+        return [DRIFT + 4 * c + q for q in range(4)]
+
+    def edge_rows(c):
+        return [c, ROWS - DRIFT + c]
+
+    for k in range(1, nlon + 1):
+        pick_rows(east(k % nlon), k, middle_rows(east(k % nlon)), 0, (0, 0, 0, 0))
     pl.semaphore_wait(barrier, greeted)
-
-    b_tile, b_rows, b_put = vector(0)
-    waiting = [start_exchange(diag_tile, diag_rows, 0), start_exchange(b_tile, b_rows, 1)]
-    finish_exchange(waiting[0], diag_put, 0)
+    beside = [
+        remote.start(inner.at[:, :, pl.ds(ROWS - DRIFT, DRIFT), :], upper.at[:, :, pl.ds(0, DRIFT), :], lon, north(1)),
+        remote.start(inner.at[:, :, pl.ds(0, DRIFT), :], lower.at[:, :, pl.ds(2 * DRIFT, DRIFT), :], lon, north(-1)),
+    ]
+
+    def send_picked(start, size):
+        return [
+            remote.start(
+                picked.at[k - 1, pl.ds(start, size)], gathered.at[lon, pl.ds(start, size)], east(k), lat
+            )
+            for k in range(1, nlon)
+        ]
+
+    sent_middle = send_picked(0, 64)
+    own[0].wait()
+    diag_waiting = start_exchange(diag_tile, diag_rows, 0)
+    for copy in own[5:]:
+        copy.wait()
+    for copy in beside:
+        copy.wait_recv()
+    for k in range(1, nlon + 1):
+        pick_rows(east(k % nlon), k, edge_rows(east(k % nlon)), 64, (1, 2))
+    sent_edge = send_picked(64, 32)
+
+    finish_exchange(diag_waiting, diag_put, 0)
+    remote.settle(diag_waiting)
 
     def shift_diag(level, carry):
         add = 4.0 + 2.0 * vertical[level] - middle
         dd[level] = wide(double, (XR, XC)) * (dd[level] + add)
         return carry
 
-    remote.drain()
-    remote.all.clear()
     lax.fori_loop(0, 4, shift_diag, 0)
+
+    first_half = sub < 4
+    lanes = iota((32, 128), 1)
+
+    def band_rows(pp, j):
+        low = pl.multiple_of(pp * 8, 8)
+        for m in range(4):
+            a, b = gathered[2 * m, pl.ds(low, 8), :], gathered[2 * m + 1, pl.ds(low, 8), :]
+            pair = (
+                jnp.where(first_half, a, pltpu.roll(b, 4, 0)),
+                jnp.where(first_half, pltpu.roll(a, 4, 0), b),
+            )
+            for n in range(2):
+                circle[2 * pp + n, 8 + 8 * m : 16 + 8 * m, :] = pair[n]
+                circle[2 * pp + n, 40 + 8 * m : 48 + 8 * m, :] = pair[n]
+                if m == 3:
+                    circle[2 * pp + n, 0:8, :] = pair[n]
+                if m == 0:
+                    circle[2 * pp + n, 72:80, :] = pair[n]
+        start = 8 + lax.rem(64 - shifts[j], 32)
+        kind = classes[j]
+        outs = []
+        for n in range(2):
+            now = circle[2 * pp + n, pl.ds(start, 32), :]
+            before = circle[2 * pp + n, pl.ds(start - 1, 32), :]
+            after = circle[2 * pp + n, pl.ds(start + 1, 32), :]
+            total = band[kind, 0] * pltpu.roll(jnp.where(lanes == 127, before, now), 1, 1)
+            total = total + band[kind, 1] * now
+            total = total + band[kind, 2] * pltpu.roll(jnp.where(lanes == 0, after, now), 127, 1)
+            total = total + band[kind, 3] * pltpu.roll(jnp.where(lanes < 2, after, now), 126, 1)
+            outs.append(total)
+        for m in range(4):
+            a, b = outs[0][8 * m : 8 * m + 8], outs[1][8 * m : 8 * m + 8]
+            banded[2 * m, pl.ds(low, 8), :] = jnp.where(first_half, a, pltpu.roll(b, 4, 0))
+            banded[2 * m + 1, pl.ds(low, 8), :] = jnp.where(first_half, pltpu.roll(a, 4, 0), b)
+
+    def middle_band(pp, carry):
+        band_rows(pp, DRIFT + 4 * lon + pp // 2)
+        return carry
+
+    def edge_band(pp, carry):
+        band_rows(pp, lon + (ROWS - DRIFT) * ((pp - 8) // 2))
+        return carry
+
+    def send_banded(start, size):
+        here = pl.multiple_of(lon * 96 + start, 8)
+        copies = [
+            remote.start(banded.at[east(k), pl.ds(start, size)], returned.at[pl.ds(here, size)], east(k), lat)
+            for k in range(1, nlon)
+        ]
+        returned[pl.ds(here, size), :] = banded[lon, pl.ds(start, size), :]
+        return copies
+
+    for copy in sent_middle:
+        copy.wait_recv()
+    lax.fori_loop(0, 8, middle_band, 0)
+    back_middle = send_banded(0, 64)
+    for copy in sent_edge:
+        copy.wait_recv()
+    lax.fori_loop(8, 12, edge_band, 0)
+    back_edge = send_banded(64, 32)
+    for copy in back_middle + back_edge:
+        copy.wait_recv()
+    b_tile, b_rows, b_put = vector(0)
+    for level in range(4):
+        for b in range(4):
+            place = 4 * level + b
+            for t in range(6):
+                if t in (0, 5):
+                    tile = returned[pl.ds(64 + 16 * (t // 5) + place, 8, stride=96), :]
+                else:
+                    tile = jnp.concatenate(
+                        [returned[pl.ds((2 * t - 2 + n) * 96 + place, 4, stride=16), :] for n in range(2)], 0
+                    )
+                b_put(level, t, b, tile)
+                dep[level, 8 * t : 8 * t + 8, 128 * b : 128 * b + 128] = tile
+    waiting = [None, start_exchange(b_tile, b_rows, 1)]
     finish_exchange(waiting[1], b_put, 1)
     build(0, STEPS + 1)
     answer, direction, residual, worst = coefficients(gram(STEPS + 1, 0, True), STEPS, middle, half, False)
+    remote.settle(waiting[1])
     combine(
         STEPS + 1,
         [(answer, put_out), (direction, put_vector(0)), (residual, put_vector(STEPS + 1))],
@@ -418,19 +539,26 @@
     remote.drain()
 
 
-def solve(departure, helm_diag, vertical, nlon, nlat):
-    copies = 4 * 8 + 2 * (nlon - 1 + nlat - 1)
+def solve(source_field, helm_diag, vertical, band, offsets, shifts, classes, nlon, nlat):
+    copies = 2 + 4 * (nlon - 1) + 4 * 8 + 2 * (nlon - 1 + nlat - 1)
     vmem = pl.BlockSpec(memory_space=pltpu.VMEM)
+    smem = pl.BlockSpec(memory_space=pltpu.SMEM)
     anywhere = pl.BlockSpec(memory_space=pl.ANY)
+    field = jax.ShapeDtypeStruct(source_field.shape, F32)
     return pl.pallas_call(
         partial(solve_kernel, nlon, nlat),
-        out_shape=(
-            jax.ShapeDtypeStruct(departure.shape, F32),
-            jax.ShapeDtypeStruct((8, 128), F32),
-        ),
-        in_specs=[pl.BlockSpec(memory_space=pltpu.SMEM), anywhere, anywhere],
-        out_specs=(vmem, vmem),
+        out_shape=(field, field, jax.ShapeDtypeStruct((8, 128), F32)),
+        in_specs=[smem] * 5 + [anywhere, anywhere],
+        out_specs=(vmem, vmem, vmem),
         scratch_shapes=[
+            pltpu.VMEM((4, 4, ROWS, 128), F32),
+            pltpu.VMEM((4, 4, 3 * DRIFT, 128), F32),
+            pltpu.VMEM((4, 4, 3 * DRIFT, 128), F32),
+            pltpu.VMEM((nlon - 1, 96, 128), F32),
+            pltpu.VMEM((nlon, 96, 128), F32),
+            pltpu.VMEM((24, 80, 128), F32),
+            pltpu.VMEM((nlon, 96, 128), F32),
+            pltpu.VMEM((nlon * 96, 128), F32),
             pltpu.VMEM((2 * STEPS + 1, 6, XR, XC), F32),
             pltpu.VMEM((4, XR, XC), F32),
             pltpu.VMEM((4, 2, 4, 8, COLS), F32),
@@ -439,7 +567,7 @@
             pltpu.VMEM((128, 128), F32),
             pltpu.VMEM((2, nlon, 8, 128), F32),
             pltpu.VMEM((2, nlat, 8, 128), F32),
-            pltpu.SemaphoreType.DMA((2,)),
+            pltpu.SemaphoreType.DMA((13,)),
             pltpu.SemaphoreType.DMA((copies,)),
             pltpu.SemaphoreType.DMA((copies,)),
         ],
@@ -447,7 +575,7 @@
             collective_id=0, has_side_effects=True, vmem_limit_bytes=40 * 1024 * 1024
         ),
         name="solve",
-    )(vertical, departure, helm_diag)
+    )(vertical, band, offsets, shifts, classes, source_field, helm_diag)
 
 
 def iterate(departure, helm_diag, vertical):
@@ -467,31 +595,10 @@
 
 
 def body(source_field, helm_diag, vertical, cubic_band, lat_offset, zonal_shift, row_class):
-    levels, lat_rows, lon_cells = source_field.shape
-    lon_count = lax.axis_size("lon")
-    total_lon = lon_cells * lon_count
-    blocks = jnp.mod(zonal_shift, total_lon // 128)
-    row_table = jnp.dot(
-        jax.nn.one_hot(row_class, cubic_band.shape[0], dtype=jnp.float32),
-        cubic_band,
-        precision=lax.Precision.HIGHEST,
+    departure, quick, worst = solve(
+        source_field, helm_diag, vertical, cubic_band, lat_offset, zonal_shift, row_class,
+        lax.axis_size("lon"), lax.axis_size("lat"),
     )
-    padded = with_halo(source_field, (("lat", 1),), DRIFT, False)
-    picked = jnp.take(padded, jnp.arange(lat_rows, dtype=jnp.int32) + DRIFT + lat_offset, axis=1)
-    per_device = lon_cells // 128
-    device_steps = (blocks // per_device)[None, :, None]
-    remain = blocks % per_device
-
-    def advance(counter, carry):
-        current, result = carry
-        current = shifted(current, "lon", 1)
-        result = jnp.where(device_steps == counter, current, result)
-        return (current, result)
-
-    moved = lax.fori_loop(1, lon_count, advance, (picked, picked))[1]
-    framed = with_halo(moved, (("lon", 2),), lon_cells, True)
-    departure = finish(framed, remain, row_table, lon_cells)
-    quick, worst = solve(departure, helm_diag, vertical, lon_count, lax.axis_size("lat"))
     answer = lax.cond(
         worst[0, 0] < LIMIT, lambda *_: quick, iterate, departure, helm_diag, vertical
     )

time: 283 us -> 71.3 us (0.25)
  local copies, waits for them, and re-layouts: 118 us -> 3.8 us
  waiting for transfers between devices: 79.9 us -> 0 us
  starting transfers between devices: 11.9 us -> 0 us
  other arithmetic: 3.65 us -> 0 us
    ppermute x11 -> x0, waiting for transfers between devices: 79.9 us -> none  [the longest x7 74.3 us: shifted(): return lax.ppermute(x, axis, [(i, (i + by) % peers) for i in range(peers)])]
    slice x2 -> x0, local copies, waits for them, and re-layouts: 33.2 us -> none  [the longest x1 33.2 us: band_row(): summed = weights[0] * window[:, 0:length]]
    unnamed x17 -> x15, local copies, waits for them, and re-layouts: 32.7 us -> 3.28 us
    gather x2 -> x0, local copies, waits for them, and re-layouts: 28 us -> none  [the longest x1 27.2 us: band_row(): window = lax.dynamic_slice_in_dim(row_cells, begin_at, length + 3, 1)]
    concatenate x1 -> x0, local copies, waits for them, and re-layouts: 23.6 us -> none  [with_halo(): jnp.concatenate([lax.ppermute(tail, axis, [(i, (i + 1) % count) for i in...]
    ppermute x11 -> x0, starting transfers between devices: 11.9 us -> none  [the longest x2 6.89 us: with_halo(): lax.ppermute(head, axis, [((i + 1) % count, i) for i in range(ends)])]
  transfers between devices with their start and end apart: 11 -> 0, of which waited for: 8 -> 0; matrix products, arithmetic and copies ran while one was open for 1% -> 0% of each run, Pallas kernels for 0% -> 0%
where the time goes in v2:
time: 71.3 us; the launch traced here: 71.1 us
  Pallas kernels  65.9 us (92%)
  local copies, waits for them, and re-layouts  3.8 us (5%)
  between operations  1.36 us (2%)
    pallas_call x1, Pallas kernels, solve(): pl.pallas_call(partial(solve_kernel, nlon, nlat), out_shape=(field, field...  65.9 us
    unnamed x15, local copies, waits for them, and re-layouts  3.28 us

profile of v2, /device:TPU:1, one launch (start us, length us, event | category | flops | bytes accessed | tf_op | source)
XLA Modules:
  0.0 71.1 jit_solution(9504920138279599078)
XLA Ops:
  0.6 0.0 copy-start.5
  0.6 0.0 copy-start.1
  0.7 0.0 copy-start.2
  0.7 0.0 copy-start.3
  0.7 0.8 %copy.9.band = f32[8,4]{1,0:T(8,128)S(1)} copy(f32[8,4]{0,1:T(4,128)} %param.14) | data formatting | bytes 256 | tf_op args[3]
  1.5 0.0 copy-done.5
  1.5 0.0 copy-done.1
  1.5 0.0 copy-done.2
  1.5 0.0 copy-done.3
  1.5 0.0 copy-start
  1.5 1.0 %copy-done = f32[4,48,512]{2,1,0:T(8,128)S(1)} copy-done((f32[4,48,512]{2,1,0:T(8,128)S(1)}, f32[4,48,512]{2,1,0:T(8,128)}, u32[]{:S(2)}) %copy-start) | copy-done | bytes 393240
  2.5 0.0 copy-start.4
  2.5 65.9 %solve.1 = (f32[4,48,512]{2,1,0:T(8,128)S(1)}, f32[4,48,512]{2,1,0:T(8,128)S(1)}, f32[8,128]{1,0:T(8,128)S(1)}) custom-call(f32[4]{0:T(128)S(1)} %copy-done.5, f32[8,4]{1,0:T(8,128)S(1)} %copy.9.band, s32[48]{0:T(128)S(1)} %copy-done.1, s32[48]{0:T(128)S(1)} %copy-done.2, s32[48]{0:T(128)S(1)} %copy-done.3, f32[4,48,512]{2,1,0:T(8,128)S(1)} %copy-done, ...), custom_call_target="tpu_custom_call" | custom-call | tf_op jit(solution)/shard_map/solve/pallas_call | solution.py:548
  68.4 0.5 slice.101
  69.6 0.0 copy-done.4
  69.6 0.7 %copy.29 = f32[4,48,512]{2,1,0:T(8,128)} copy(f32[4,48,512]{2,1,0:T(8,128)S(1)} %get-tuple-element.256) | data formatting | bytes 786432
  70.4 0.7 %copy.30 = f32[4,48,512]{2,1,0:T(8,128)} copy(f32[4,48,512]{2,1,0:T(8,128)S(1)} %get-tuple-element.258) | data formatting | bytes 786432
  (1 shorter events, 0.0 us)
Async XLA Ops:
  0.6 0.8 %copy-start.5 = (f32[4]{0:T(128)S(1)}, f32[4]{0:T(128)}, u32[]{:S(2)}) copy-start(f32[4]{0:T(128)} %vertical.1) | copy-start | bytes 52
  0.6 0.8 %copy-start.1 = (s32[48]{0:T(128)S(1)}, s32[48]{0:T(128)}, u32[]{:S(2)}) copy-start(s32[48]{0:T(128)} %offsets.1) | copy-start | bytes 580
  0.7 0.8 %copy-start.2 = (s32[48]{0:T(128)S(1)}, s32[48]{0:T(128)}, u32[]{:S(2)}) copy-start(s32[48]{0:T(128)} %shifts.1) | copy-start | bytes 580
  0.7 0.8 %copy-start.3 = (s32[48]{0:T(128)S(1)}, s32[48]{0:T(128)}, u32[]{:S(2)}) copy-start(s32[48]{0:T(128)} %classes.1) | copy-start | bytes 580
  1.5 1.0 %copy-start = (f32[4,48,512]{2,1,0:T(8,128)S(1)}, f32[4,48,512]{2,1,0:T(8,128)}, u32[]{:S(2)}) copy-start(f32[4,48,512]{2,1,0:T(8,128)} %source.1) | copy-start | bytes 1179652
  2.5 67.1 %copy-start.4 = (f32[4,48,512]{2,1,0:T(8,128)S(1)}, f32[4,48,512]{2,1,0:T(8,128)}, u32[]{:S(2)}) copy-start(f32[4,48,512]{2,1,0:T(8,128)} %helm.1) | copy-start | bytes 1179652

commit v3 on v2

--- a/solution.py
+++ b/solution.py
@@ -51,11 +51,10 @@
 
 MESH = pl.DeviceIdType.MESH
 F32 = jnp.float32
-STEPS = 4
-LOW, REST = 0.05, 9.0
+STEPS = 8
 LIMIT = 1.5e4
 ROWS, COLS = 48, 512
-XR, XC = 56, 640
+XR, XC = 64, 640
 
 
 def iota(shape, dim):
@@ -90,10 +89,7 @@
             copy.wait_send()
 
 
-def coefficients(gram, steps, middle, half, final):
-    shared = gram.shared
-    base = 0 if shared else steps + 1
-
+def coefficients(gram, steps, middle, half):
     def apply(vec):
         out = {}
 
@@ -101,10 +97,9 @@
             out[i] = out[i] + x if i in out else x
 
         for i, x in vec.items():
-            start = 0 if i <= steps else steps + 1
             add(i, x * middle)
-            if i == start:
-                add(i + 1, x * half)
+            if i == 0:
+                add(1, x * half)
             else:
                 add(i + 1, x * (0.5 * half))
                 add(i - 1, x * (0.5 * half))
@@ -126,26 +121,26 @@
         return {i: a[i] + scale * b[i] if i in a and i in b else (a[i] if i in a else scale * b[i]) for i in {**a, **b}}
 
     one = jnp.ones((8, 128), F32)
-    direction, residual, answer = {0: one}, {base: one}, {}
-    norm, worst = gram(base, base), one
+    direction, residual, answer = {0: one}, {0: one}, {}
+    norm, worst = gram(0, 0), one
     for count in range(steps):
         applied = apply(direction)
         slope, size = form(direction, applied)
         worst = jnp.maximum(worst, size)
         rate = norm / slope
         answer = plus(answer, rate, direction)
-        if not (final and count == steps - 1):
+        if count < steps - 1:
             residual = plus(residual, -rate, applied)
             follow, size = form(residual, residual)
             worst = jnp.maximum(worst, size)
             direction = plus(residual, follow / norm, direction)
             norm = follow
-    return answer, direction, residual, worst
+    return answer, worst
 
 
 class Gram:
-    def __init__(self, row, pairs, shared):
-        self.row, self.place, self.shared, self.cache = row, {p: i for i, p in enumerate(pairs)}, shared, {}
+    def __init__(self, row, pairs):
+        self.row, self.place, self.cache = row, {p: i for i, p in enumerate(pairs)}, {}
 
     def __call__(self, i, j):
         pair = (min(i, j), max(i, j))
@@ -158,7 +153,7 @@
 def solve_kernel(
     nlon, nlat, vertical, band, offsets, shifts, classes, source, helm, dep, out, flag,
     inner, upper, lower, picked, gathered, circle, banded, returned,
-    vs, dd, lat_in, lon_in, packs, stage, slot_lon, slot_lat, local_sems, send_sems, recv_sems,
+    vs, dd, lon_in, packs, stage, slot_lon, slot_lat, local_sems, send_sems, recv_sems,
 ):
     lon, lat = lax.axis_index("lon"), lax.axis_index("lat")
 
@@ -202,27 +197,29 @@
     top_ok, bottom_ok = lat > 0, lat < nlat - 1
 
     zero = jnp.zeros((XR, XC), F32)
-    for j in range(2 * STEPS + 1):
+    for j in range(STEPS + 1):
         vs[j, 0] = zero
         vs[j, 5] = zero
     stage[...] = jnp.zeros_like(stage)
 
-    biggest = jnp.maximum(jnp.maximum(vertical[0], vertical[1]), jnp.maximum(vertical[2], vertical[3]))
-    top = REST + 4.0 * biggest
-    middle, half = 0.5 * (top + LOW), 0.5 * (top - LOW)
-    double = (jnp.full((8, 128), 2.0, F32) / jnp.broadcast_to(half, (8, 128)))
-
-    def start_exchange(tile, rows, which):
-        right = left = jnp.zeros((8, 128), F32)
-        for i in range(24):
-            here = lane // 4 == i
-            right = jnp.where(here, pltpu.roll(tile(i // 6, i % 6, 3), (4 * i + 4) % 128, 1), right)
-            left = jnp.where(here, pltpu.roll(tile(i // 6, i % 6, 0), (4 * i) % 128, 1), left)
-        packs[which, 0] = right
-        packs[which, 1] = left
+    mean = 0.25 * ((vertical[0] + vertical[1]) + (vertical[2] + vertical[3]))
+    top = 0.9 * (9.0 + 4.0 * mean)
+    middle, half = 0.54 * top, 0.46 * top
+    double = jnp.full((8, 128), 2.0, F32) / jnp.broadcast_to(half, (8, 128))
+
+    def start_exchange(tile, place, which):
+        for h in range(2):
+            right = left = jnp.zeros((8, 128), F32)
+            for i in range(12):
+                here = lane // 8 == i
+                level = 2 * h + i // 6
+                right = jnp.where(here, pltpu.roll(tile(level, i % 6, 3), (8 * i + 8) % 128, 1), right)
+                left = jnp.where(here, pltpu.roll(tile(level, i % 6, 0), 8 * i, 1), left)
+            packs[which, 0, h] = right
+            packs[which, 1, h] = left
         return [
-            remote.start(rows(40), lat_in.at[which, 0], lon, north(1)),
-            remote.start(rows(0), lat_in.at[which, 1], lon, north(-1)),
+            remote.start(place(ROWS - 8), place(ROWS + 8), lon, north(1)),
+            remote.start(place(0), place(ROWS), lon, north(-1)),
             remote.start(packs.at[which, 0], lon_in.at[which, 0], east(1), lat),
             remote.start(packs.at[which, 0], lon_in.at[which, 1], east(1), north(1)),
             remote.start(packs.at[which, 0], lon_in.at[which, 2], east(1), north(-1)),
@@ -234,33 +231,21 @@
     def finish_exchange(copies, put, which):
         for copy in copies:
             copy.wait_recv()
-        ok = jnp.where(sub < 4, bottom_ok.astype(jnp.int32), top_ok.astype(jnp.int32)) > 0
-        packed = [lon_in[which, i] for i in range(6)]
         for level in range(4):
-            for t in range(7):
-                if t < 6:
-                    i = level * 6 + t
-                    west, east_ = packed[0], packed[3]
-                    westward = pltpu.roll(west, (124 - 4 * i) % 128, 1)
-                    eastward = pltpu.roll(east_, (-4 * i) % 128, 1)
-                    put(level, t, 4, jnp.where(lane < 64, eastward, westward))
-                else:
-                    first, last = level * 6, level * 6 + 5
-                    westward = jnp.where(
-                        sub < 4,
-                        pltpu.roll(packed[2], (124 - 4 * first) % 128, 1),
-                        pltpu.roll(packed[1], (124 - 4 * last) % 128, 1),
-                    )
-                    eastward = jnp.where(
-                        sub < 4,
-                        pltpu.roll(packed[5], (-4 * first) % 128, 1),
-                        pltpu.roll(packed[4], (-4 * last) % 128, 1),
-                    )
-                    put(level, t, 4, jnp.where(ok, jnp.where(lane < 64, eastward, westward), 0.0))
-            for b in range(4):
-                above = lat_in[which, 0, level, :, 128 * b : 128 * b + 128]
-                below = lat_in[which, 1, level, :, 128 * b : 128 * b + 128]
-                put(level, 6, b, jnp.where(ok, jnp.where(sub < 4, below, above), 0.0))
+            packed = [lon_in[which, i, level // 2] for i in range(6)]
+            for t in range(8):
+                i = 6 * (level % 2) + (t if t < 6 else 0 if t == 6 else 5)
+                side = 0 if t < 6 else 2 if t == 6 else 1
+                westward = pltpu.roll(packed[side], (120 - 8 * i) % 128, 1)
+                eastward = pltpu.roll(packed[3 + side], (-8 * i) % 128, 1)
+                put(level, t, 4, jnp.where(lane < 64, eastward, westward))
+        for missing, t in ((lat == nlat - 1, 6), (lat == 0, 7)):
+
+            @pl.when(missing)
+            def _(t=t):
+                for level in range(4):
+                    for b in range(5):
+                        put(level, t, b, jnp.zeros((8, 128), F32))
 
     def vector(j):
         def tile(level, t, b):
@@ -287,7 +272,7 @@
         return jnp.broadcast_to(x[0:1, 0:1], shape)
 
     def chebyshev(src, before, dst):
-        mask = jnp.where(iota((8, XC), 0) < 4, bottom_ok.astype(F32), top_ok.astype(F32))
+        mask = jnp.where(iota((16, XC), 0) < 8, bottom_ok.astype(F32), top_ok.astype(F32))
         scale = wide(double, (XR, XC))
 
         def one(level, carry):
@@ -307,29 +292,30 @@
         for k in range(1, count):
             chebyshev(base + k - 1, None if k == 1 else base + k - 2, base + k)
 
-    def all_reduce(value, turn):
-        slot_lon[turn, lon] = value
+    def all_reduce(value):
+        slot_lon[lon] = value
         copies = [
-            remote.start(slot_lon.at[turn, lon], slot_lon.at[turn, lon], east(k), lat) for k in range(1, nlon)
+            remote.start(slot_lon.at[lon], slot_lon.at[lon], east(k), lat) for k in range(1, nlon)
         ]
         for copy in copies:
             copy.wait_recv()
-        value = slot_lon[turn, 0]
+        value = slot_lon[0]
         for i in range(1, nlon):
-            value = value + slot_lon[turn, i]
-        slot_lat[turn, lat] = value
+            value = value + slot_lon[i]
+        slot_lat[lat] = value
         copies = [
-            remote.start(slot_lat.at[turn, lat], slot_lat.at[turn, lat], lon, north(k)) for k in range(1, nlat)
+            remote.start(slot_lat.at[lat], slot_lat.at[lat], lon, north(k)) for k in range(1, nlat)
         ]
         for copy in copies:
             copy.wait_recv()
-        value = slot_lat[turn, 0]
+        value = slot_lat[0]
         for i in range(1, nlat):
-            value = value + slot_lat[turn, i]
+            value = value + slot_lat[i]
         return value
 
-    def gram(count, turn, shared):
-        pairs = [(i, j) for i in range(count) for j in range(i, count)]
+    def gram():
+        count = STEPS + 1
+        pairs = [(i, j) for i in range(count) for j in range(i, count) if i < STEPS]
 
         def one(t, sums):
             level, r = t // 6, pl.multiple_of((t % 6) * 8, 8)
@@ -347,36 +333,20 @@
             jnp.ones((8, 128), F32), stage[...], (((1,), (1,)), ((), ())),
             precision=lax.Precision.HIGHEST, preferred_element_type=F32,
         )
-        return Gram(all_reduce(row, turn), pairs, shared)
-
-    def combine(count, outputs):
+        return Gram(all_reduce(row), pairs)
+
+    def combine(coef):
         def one(t, carry):
             level, r = t // 6, pl.multiple_of((t % 6) * 8, 8)
             for b in range(4):
-                tiles = [vs[i, level + 1, pl.ds(r, 8), 128 * b : 128 * b + 128] for i in range(count)]
-                values = []
-                for coef, _ in outputs:
-                    value = None
-                    for i, x in coef.items():
-                        value = x * tiles[i] if value is None else value + x * tiles[i]
-                    values.append(value)
-                for value, (_, write) in zip(values, outputs):
-                    write(level, pl.ds(r, 8), pl.ds(128 * b, 128), value)
+                value = None
+                for i, x in coef.items():
+                    term = x * vs[i, level + 1, pl.ds(r, 8), 128 * b : 128 * b + 128]
+                    value = term if value is None else value + term
+                out[level, pl.ds(r, 8), 128 * b : 128 * b + 128] = value
             return carry
 
         lax.fori_loop(0, 24, one, 0)
-
-    def put_out(level, r, b, value):
-        out[level, r, b] = value
-
-    def add_out(level, r, b, value):
-        out[level, r, b] = out[level, r, b] + value
-
-    def put_vector(j):
-        def write(level, r, b, value):
-            vs[j, level + 1, r, b] = value
-
-        return write
 
     for copy in own[1:5]:
         copy.wait()
@@ -517,30 +487,18 @@
                     )
                 b_put(level, t, b, tile)
                 dep[level, 8 * t : 8 * t + 8, 128 * b : 128 * b + 128] = tile
-    waiting = [None, start_exchange(b_tile, b_rows, 1)]
-    finish_exchange(waiting[1], b_put, 1)
-    build(0, STEPS + 1)
-    answer, direction, residual, worst = coefficients(gram(STEPS + 1, 0, True), STEPS, middle, half, False)
-    remote.settle(waiting[1])
-    combine(
-        STEPS + 1,
-        [(answer, put_out), (direction, put_vector(0)), (residual, put_vector(STEPS + 1))],
-    )
-    p_tile, p_rows, p_put = vector(0)
-    r_tile, r_rows, r_put = vector(STEPS + 1)
-    waiting = [start_exchange(p_tile, p_rows, 2), start_exchange(r_tile, r_rows, 3)]
-    finish_exchange(waiting[0], p_put, 2)
-    build(0, STEPS + 1)
-    finish_exchange(waiting[1], r_put, 3)
-    build(STEPS + 1, STEPS)
-    answer, _, _, second = coefficients(gram(2 * STEPS + 1, 1, False), STEPS, middle, half, True)
-    combine(2 * STEPS + 1, [(answer, add_out)])
-    flag[...] = jnp.maximum(worst, second)
+    waiting = start_exchange(b_tile, b_rows, 1)
+    finish_exchange(waiting, b_put, 1)
+    for k in range(1, STEPS + 1):
+        chebyshev(k - 1, None if k == 1 else k - 2, k)
+    answer, worst = coefficients(gram(), STEPS, middle, half)
+    combine(answer)
+    flag[...] = worst
     remote.drain()
 
 
 def solve(source_field, helm_diag, vertical, band, offsets, shifts, classes, nlon, nlat):
-    copies = 2 + 4 * (nlon - 1) + 4 * 8 + 2 * (nlon - 1 + nlat - 1)
+    copies = 2 + 4 * (nlon - 1) + 2 * 8 + (nlon - 1 + nlat - 1)
     vmem = pl.BlockSpec(memory_space=pltpu.VMEM)
     smem = pl.BlockSpec(memory_space=pltpu.SMEM)
     anywhere = pl.BlockSpec(memory_space=pl.ANY)
@@ -559,14 +517,13 @@
             pltpu.VMEM((24, 80, 128), F32),
             pltpu.VMEM((nlon, 96, 128), F32),
             pltpu.VMEM((nlon * 96, 128), F32),
-            pltpu.VMEM((2 * STEPS + 1, 6, XR, XC), F32),
+            pltpu.VMEM((STEPS + 1, 6, XR, XC), F32),
             pltpu.VMEM((4, XR, XC), F32),
-            pltpu.VMEM((4, 2, 4, 8, COLS), F32),
-            pltpu.VMEM((4, 6, 8, 128), F32),
-            pltpu.VMEM((4, 2, 8, 128), F32),
+            pltpu.VMEM((2, 6, 2, 8, 128), F32),
+            pltpu.VMEM((2, 2, 2, 8, 128), F32),
             pltpu.VMEM((128, 128), F32),
-            pltpu.VMEM((2, nlon, 8, 128), F32),
-            pltpu.VMEM((2, nlat, 8, 128), F32),
+            pltpu.VMEM((nlon, 8, 128), F32),
+            pltpu.VMEM((nlat, 8, 128), F32),
             pltpu.SemaphoreType.DMA((13,)),
             pltpu.SemaphoreType.DMA((copies,)),
             pltpu.SemaphoreType.DMA((copies,)),

time: 71.3 us -> 52.6 us (0.74)
  Pallas kernels: 65.9 us -> 47.3 us
    pallas_call x1, Pallas kernels: 65.9 us -> 47.3 us  [solve(): pl.pallas_call(partial(solve_kernel, nlon, nlat), out_shape=(field, field...]
where the time goes in v3:
time: 52.6 us; the launch traced here: 52.5 us
  Pallas kernels  47.3 us (90%)
  local copies, waits for them, and re-layouts  3.8 us (7%)
  between operations  1.36 us (3%)
    pallas_call x1, Pallas kernels, solve(): pl.pallas_call(partial(solve_kernel, nlon, nlat), out_shape=(field, field...  47.3 us
    unnamed x15, local copies, waits for them, and re-layouts  3.28 us

profile of v3, /device:TPU:1, one launch (start us, length us, event | category | flops | bytes accessed | tf_op | source)
XLA Modules:
  0.0 52.5 jit_solution(15987540009642976115)
XLA Ops:
  0.6 0.0 copy-start.5
  0.6 0.0 copy-start.1
  0.7 0.0 copy-start.2
  0.7 0.0 copy-start.3
  0.7 0.8 %copy.9.band = f32[8,4]{1,0:T(8,128)S(1)} copy(f32[8,4]{0,1:T(4,128)} %param.14) | data formatting | bytes 256 | tf_op args[3]
  1.5 0.0 copy-done.5
  1.5 0.0 copy-done.1
  1.5 0.0 copy-done.2
  1.5 0.0 copy-done.3
  1.5 0.0 copy-start
  1.5 1.0 %copy-done = f32[4,48,512]{2,1,0:T(8,128)S(1)} copy-done((f32[4,48,512]{2,1,0:T(8,128)S(1)}, f32[4,48,512]{2,1,0:T(8,128)}, u32[]{:S(2)}) %copy-start) | copy-done | bytes 393240
  2.5 0.0 copy-start.4
  2.5 47.3 %solve.1 = (f32[4,48,512]{2,1,0:T(8,128)S(1)}, f32[4,48,512]{2,1,0:T(8,128)S(1)}, f32[8,128]{1,0:T(8,128)S(1)}) custom-call(f32[4]{0:T(128)S(1)} %copy-done.5, f32[8,4]{1,0:T(8,128)S(1)} %copy.9.band, s32[48]{0:T(128)S(1)} %copy-done.1, s32[48]{0:T(128)S(1)} %copy-done.2, s32[48]{0:T(128)S(1)} %copy-done.3, f32[4,48,512]{2,1,0:T(8,128)S(1)} %copy-done, ...), custom_call_target="tpu_custom_call" | custom-call | tf_op jit(solution)/shard_map/solve/pallas_call | solution.py:506
  49.8 0.5 slice.101
  50.9 0.0 copy-done.4
  51.0 0.7 %copy.29 = f32[4,48,512]{2,1,0:T(8,128)} copy(f32[4,48,512]{2,1,0:T(8,128)S(1)} %get-tuple-element.256) | data formatting | bytes 786432
  51.7 0.7 %copy.30 = f32[4,48,512]{2,1,0:T(8,128)} copy(f32[4,48,512]{2,1,0:T(8,128)S(1)} %get-tuple-element.258) | data formatting | bytes 786432
  (1 shorter events, 0.0 us)
Async XLA Ops:
  0.6 0.8 %copy-start.5 = (f32[4]{0:T(128)S(1)}, f32[4]{0:T(128)}, u32[]{:S(2)}) copy-start(f32[4]{0:T(128)} %vertical.1) | copy-start | bytes 52
  0.6 0.8 %copy-start.1 = (s32[48]{0:T(128)S(1)}, s32[48]{0:T(128)}, u32[]{:S(2)}) copy-start(s32[48]{0:T(128)} %offsets.1) | copy-start | bytes 580
  0.7 0.8 %copy-start.2 = (s32[48]{0:T(128)S(1)}, s32[48]{0:T(128)}, u32[]{:S(2)}) copy-start(s32[48]{0:T(128)} %shifts.1) | copy-start | bytes 580
  0.7 0.8 %copy-start.3 = (s32[48]{0:T(128)S(1)}, s32[48]{0:T(128)}, u32[]{:S(2)}) copy-start(s32[48]{0:T(128)} %classes.1) | copy-start | bytes 580
  1.5 1.0 %copy-start = (f32[4,48,512]{2,1,0:T(8,128)S(1)}, f32[4,48,512]{2,1,0:T(8,128)}, u32[]{:S(2)}) copy-start(f32[4,48,512]{2,1,0:T(8,128)} %source.1) | copy-start | bytes 1179652
  2.5 48.5 %copy-start.4 = (f32[4,48,512]{2,1,0:T(8,128)S(1)}, f32[4,48,512]{2,1,0:T(8,128)}, u32[]{:S(2)}) copy-start(f32[4,48,512]{2,1,0:T(8,128)} %helm.1) | copy-start | bytes 1179652

commit v4 on v3

--- a/solution.py
+++ b/solution.py
@@ -1,3 +1,4 @@
+import itertools
 from functools import partial
 
 import jax
@@ -52,9 +53,11 @@
 MESH = pl.DeviceIdType.MESH
 F32 = jnp.float32
 STEPS = 8
+SIZES = {"zl": 2, "x": 4, "zh": 2, "y": 4, "c": 2}
+PLANE, REST = ("x", "y"), ("zl", "zh", "c")
 LIMIT = 1.5e4
 ROWS, COLS = 48, 512
-XR, XC = 64, 640
+XR, TOP, TILES = 80, 16, 5
 
 
 def iota(shape, dim):
@@ -153,7 +156,7 @@
 def solve_kernel(
     nlon, nlat, vertical, band, offsets, shifts, classes, source, helm, dep, out, flag,
     inner, upper, lower, picked, gathered, circle, banded, returned,
-    vs, dd, lon_in, packs, stage, slot_lon, slot_lat, local_sems, send_sems, recv_sems,
+    vs, dd, lon_in, packs, stage, slot_plane, slot_rest, local_sems, send_sems, recv_sems,
 ):
     lon, lat = lax.axis_index("lon"), lax.axis_index("lat")
 
@@ -163,44 +166,65 @@
     def north(k):
         return lax.rem(lat + (k + nlat), nlat)
 
+    here = {"zl": lon // 4, "x": lax.rem(lon, 4), "zh": lat // 8, "y": lax.rem(lat // 2, 4), "c": lax.rem(lat, 2)}
+
+    def place_of(moves):
+        spot = {a: lax.rem(v + moves.get(a, 0), SIZES[a]) for a, v in here.items()}
+        return spot["zl"] * 4 + spot["x"], spot["zh"] * 8 + spot["y"] * 2 + spot["c"]
+
+    def partners(axes):
+        moves = [dict(zip(axes, m)) for m in itertools.product(*[range(SIZES[a]) for a in axes]) if any(m)]
+        far = {"c": 0, "zl": 1, "zh": 2}
+        return sorted(moves, key=lambda m: -sum(far.get(a, 1) * min(v, SIZES[a] - v) for a, v in m.items()))
+
+    barrier = pltpu.get_barrier_semaphore()
+    greet = [(east(k), lat) for k in range(1, nlon)]
+    greet += [(lon, north(1)), (lon, north(-1))]
+    greet += [(east(a), north(b)) for a in (-1, 1) for b in (-1, 1)]
+    greet += [place_of(m) for m in partners(PLANE) if m["y"]]
+    greet += [place_of(m) for m in partners(REST) if m["zh"] or m["c"]]
+    for peer in greet:
+        pl.semaphore_signal(barrier, inc=1, device_id=peer, device_id_type=MESH)
+    greeted = len(greet)
     own = [
-        pltpu.make_async_copy(helm, dd.at[:, pl.ds(0, ROWS), pl.ds(0, COLS)], local_sems.at[0]),
-        *[
-            pltpu.make_async_copy(
-                source.at[:, pl.ds(start, size), pl.ds(128 * b, 128)],
-                into.at[:, b, pl.ds(at, size), :],
-                local_sems.at[1 + 4 * n + b],
-            )
-            for n, (into, start, at, size) in enumerate(
-                [(inner, 0, 0, ROWS), (upper, 0, DRIFT, 2 * DRIFT), (lower, ROWS - 2 * DRIFT, 0, 2 * DRIFT)]
-            )
-            for b in range(4)
-        ],
+        pltpu.make_async_copy(
+            source.at[:, pl.ds(start, size), pl.ds(128 * b, 128)],
+            into.at[:, b, pl.ds(at, size), :],
+            local_sems.at[4 * n + b],
+        )
+        for n, (into, start, at, size) in enumerate(
+            [(inner, 0, 0, ROWS), (upper, 0, DRIFT, 2 * DRIFT), (lower, ROWS - 2 * DRIFT, 0, 2 * DRIFT)]
+        )
+        for b in range(4)
     ]
-    for copy in own:
+    own_diag = [
+        pltpu.make_async_copy(
+            helm.at[:, :, pl.ds(128 * b, 128)], dd.at[:, b, pl.ds(TOP, ROWS), :], local_sems.at[12 + b]
+        )
+        for b in range(4)
+    ]
+    for copy in own + own_diag:
         copy.start()
-    barrier = pltpu.get_barrier_semaphore()
-    greeted = 0
-    for k in range(1, nlon):
-        pl.semaphore_signal(barrier, inc=1, device_id=(east(k), lat), device_id_type=MESH)
-        greeted += 1
-    for k in range(1, nlat):
-        pl.semaphore_signal(barrier, inc=1, device_id=(lon, north(k)), device_id_type=MESH)
-        greeted += 1
-    for a in (-1, 1):
-        for b in (-1, 1):
-            pl.semaphore_signal(barrier, inc=1, device_id=(east(a), north(b)), device_id_type=MESH)
-            greeted += 1
 
     remote = Remote(send_sems, recv_sems)
     lane, sub = iota((8, 128), 1), iota((8, 128), 0)
     top_ok, bottom_ok = lat > 0, lat < nlat - 1
 
-    zero = jnp.zeros((XR, XC), F32)
-    for j in range(STEPS + 1):
-        vs[j, 0] = zero
-        vs[j, 5] = zero
-    stage[...] = jnp.zeros_like(stage)
+    def clear():
+        zero = jnp.zeros((8, 128), F32)
+
+        def one(j, carry):
+            for b in range(TILES):
+                for t in range(XR // 8):
+                    vs[j, 0, b, 8 * t : 8 * t + 8, :] = zero
+                    vs[j, 5, b, 8 * t : 8 * t + 8, :] = zero
+                for level in range(1, 5):
+                    vs[j, level, b, 0:8, :] = zero
+                    vs[j, level, b, XR - 8 : XR, :] = zero
+            return carry
+
+        lax.fori_loop(0, STEPS + 1, one, 0)
+        stage[...] = jnp.zeros_like(stage)
 
     mean = 0.25 * ((vertical[0] + vertical[1]) + (vertical[2] + vertical[3]))
     top = 0.9 * (9.0 + 4.0 * mean)
@@ -218,8 +242,8 @@
             packs[which, 0, h] = right
             packs[which, 1, h] = left
         return [
-            remote.start(place(ROWS - 8), place(ROWS + 8), lon, north(1)),
-            remote.start(place(0), place(ROWS), lon, north(-1)),
+            remote.start(place(TOP + ROWS - 8), place(TOP - 8), lon, north(1)),
+            remote.start(place(TOP), place(TOP + ROWS), lon, north(-1)),
             remote.start(packs.at[which, 0], lon_in.at[which, 0], east(1), lat),
             remote.start(packs.at[which, 0], lon_in.at[which, 1], east(1), north(1)),
             remote.start(packs.at[which, 0], lon_in.at[which, 2], east(1), north(-1)),
@@ -233,13 +257,13 @@
             copy.wait_recv()
         for level in range(4):
             packed = [lon_in[which, i, level // 2] for i in range(6)]
-            for t in range(8):
-                i = 6 * (level % 2) + (t if t < 6 else 0 if t == 6 else 5)
-                side = 0 if t < 6 else 2 if t == 6 else 1
+            for t in range(-1, 7):
+                i = 6 * (level % 2) + (5 if t < 0 else t if t < 6 else 0)
+                side = 1 if t < 0 else 0 if t < 6 else 2
                 westward = pltpu.roll(packed[side], (120 - 8 * i) % 128, 1)
                 eastward = pltpu.roll(packed[3 + side], (-8 * i) % 128, 1)
                 put(level, t, 4, jnp.where(lane < 64, eastward, westward))
-        for missing, t in ((lat == nlat - 1, 6), (lat == 0, 7)):
+        for missing, t in ((lat == nlat - 1, 6), (lat == 0, -1)):
 
             @pl.when(missing)
             def _(t=t):
@@ -247,70 +271,81 @@
                     for b in range(5):
                         put(level, t, b, jnp.zeros((8, 128), F32))
 
-    def vector(j):
-        def tile(level, t, b):
-            return vs[j, level + 1, 8 * t : 8 * t + 8, 128 * b : 128 * b + 128]
-
-        def put(level, t, b, value):
-            vs[j, level + 1, 8 * t : 8 * t + 8, 128 * b : 128 * b + 128] = value
-
-        def rows(at):
-            return vs.at[j, pl.ds(1, 4), pl.ds(at, 8), pl.ds(0, COLS)]
-
-        return tile, rows, put
+    def b_tile(level, t, b):
+        return vs[0, level + 1, b, TOP + 8 * t : TOP + 8 * t + 8, :]
+
+    def b_put(level, t, b, value):
+        vs[0, level + 1, b, TOP + 8 * t : TOP + 8 * t + 8, :] = value
+
+    def b_rows(at):
+        return vs.at[0, pl.ds(1, 4), pl.ds(0, 4), pl.ds(at, 8), :]
 
     def diag_tile(level, t, b):
-        return dd[level, 8 * t : 8 * t + 8, 128 * b : 128 * b + 128]
+        return dd[level, b, TOP + 8 * t : TOP + 8 * t + 8, :]
 
     def diag_put(level, t, b, value):
-        dd[level, 8 * t : 8 * t + 8, 128 * b : 128 * b + 128] = value
+        dd[level, b, TOP + 8 * t : TOP + 8 * t + 8, :] = value
 
     def diag_rows(at):
-        return dd.at[:, pl.ds(at, 8), pl.ds(0, COLS)]
-
-    def wide(x, shape):
-        return jnp.broadcast_to(x[0:1, 0:1], shape)
+        return dd.at[:, pl.ds(0, 4), pl.ds(at, 8), :]
+
+    def shift_diag():
+        def one(level, carry):
+            add = 4.0 + 2.0 * vertical[level] - middle
+            for b in range(TILES):
+                for t in range(-1, 7):
+                    value = double * (diag_tile(level, t, b) + add)
+                    if t in (-1, 6):
+                        value = jnp.where(top_ok if t < 0 else bottom_ok, value, 0.0)
+                    diag_put(level, t, b, value)
+            return carry
+
+        lax.fori_loop(0, 4, one, 0)
 
     def chebyshev(src, before, dst):
-        mask = jnp.where(iota((16, XC), 0) < 8, bottom_ok.astype(F32), top_ok.astype(F32))
-        scale = wide(double, (XR, XC))
-
-        def one(level, carry):
-            mid = vs[src, level + 1]
-            sides = pltpu.roll(mid, 1, 1) + pltpu.roll(mid, XC - 1, 1)
-            sides = sides + (pltpu.roll(mid, 1, 0) + pltpu.roll(mid, XR - 1, 0))
-            stack = vs[src, level] + vs[src, level + 2]
-            value = dd[level] * mid - scale * (sides + vertical[level] * stack)
-            value = 0.5 * value if before is None else value - vs[before, level + 1]
-            vs[dst, level + 1, 0:ROWS, :] = value[0:ROWS]
-            vs[dst, level + 1, ROWS:XR, :] = value[ROWS:XR] * mask
+        last = dst == STEPS
+        first, count = (TOP, 3) if last else (TOP - 8, 4)
+
+        def one(i, carry):
+            level, pair = i // count, lax.rem(i, count)
+            for u in range(2):
+                r = pl.multiple_of(first + 16 * pair + 8 * u, 8)
+                scale = double
+                if not last and u == 0:
+                    scale = jnp.where(jnp.logical_or(pair > 0, top_ok), double, 0.0)
+                if not last and u == 1:
+                    scale = jnp.where(jnp.logical_or(pair < count - 1, bottom_ok), double, 0.0)
+                mids = [vs[src, level + 1, b, pl.ds(r, 8), :] for b in range(TILES)]
+                for b in range(4 if last else TILES):
+                    mid = mids[b]
+                    sides = pltpu.roll(jnp.where(lane == 127, mids[b - 1], mid), 1, 1)
+                    sides = sides + pltpu.roll(jnp.where(lane == 0, mids[(b + 1) % TILES], mid), 127, 1)
+                    sides = sides + (
+                        vs[src, level + 1, b, pl.ds(r - 1, 8), :] + vs[src, level + 1, b, pl.ds(r + 1, 8), :]
+                    )
+                    stack = vs[src, level, b, pl.ds(r, 8), :] + vs[src, level + 2, b, pl.ds(r, 8), :]
+                    value = dd[level, b, pl.ds(r, 8), :] * mid - scale * (sides + vertical[level] * stack)
+                    if before is None:
+                        value = 0.5 * value
+                    else:
+                        value = value - vs[before, level + 1, b, pl.ds(r, 8), :]
+                    vs[dst, level + 1, b, pl.ds(r, 8), :] = value
             return carry
 
-        lax.fori_loop(0, 4, one, 0)
-
-    def build(base, count):
-        for k in range(1, count):
-            chebyshev(base + k - 1, None if k == 1 else base + k - 2, base + k)
+        lax.fori_loop(0, 4 * count, one, 0)
 
     def all_reduce(value):
-        slot_lon[lon] = value
-        copies = [
-            remote.start(slot_lon.at[lon], slot_lon.at[lon], east(k), lat) for k in range(1, nlon)
-        ]
-        for copy in copies:
-            copy.wait_recv()
-        value = slot_lon[0]
-        for i in range(1, nlon):
-            value = value + slot_lon[i]
-        slot_lat[lat] = value
-        copies = [
-            remote.start(slot_lat.at[lat], slot_lat.at[lat], lon, north(k)) for k in range(1, nlat)
-        ]
-        for copy in copies:
-            copy.wait_recv()
-        value = slot_lat[0]
-        for i in range(1, nlat):
-            value = value + slot_lat[i]
+        for axes, slot in ((PLANE, slot_plane), (REST, slot_rest)):
+            mine = 0
+            for axis in axes:
+                mine = mine * SIZES[axis] + here[axis]
+            slot[mine] = value
+            copies = [remote.start(slot.at[mine], slot.at[mine], *place_of(m)) for m in partners(axes)]
+            for copy in copies:
+                copy.wait_recv()
+            value = slot[0]
+            for i in range(1, slot.shape[0]):
+                value = value + slot[i]
         return value
 
     def gram():
@@ -321,7 +356,7 @@
             level, r = t // 6, pl.multiple_of((t % 6) * 8, 8)
             sums = list(sums)
             for b in range(4):
-                tiles = [vs[i, level + 1, pl.ds(r, 8), 128 * b : 128 * b + 128] for i in range(count)]
+                tiles = [vs[i, level + 1, b, pl.ds(r + TOP, 8), :] for i in range(count)]
                 for n, (i, j) in enumerate(pairs):
                     sums[n] = sums[n] + tiles[i] * tiles[j]
             return tuple(sums)
@@ -341,14 +376,14 @@
             for b in range(4):
                 value = None
                 for i, x in coef.items():
-                    term = x * vs[i, level + 1, pl.ds(r, 8), 128 * b : 128 * b + 128]
+                    term = x * vs[i, level + 1, b, pl.ds(r + TOP, 8), :]
                     value = term if value is None else value + term
                 out[level, pl.ds(r, 8), 128 * b : 128 * b + 128] = value
             return carry
 
         lax.fori_loop(0, 24, one, 0)
 
-    for copy in own[1:5]:
+    for copy in own[0:4]:
         copy.wait()
 
     def pick(j, part, write):
@@ -392,9 +427,11 @@
         ]
 
     sent_middle = send_picked(0, 64)
-    own[0].wait()
+    for copy in own_diag:
+        copy.wait()
     diag_waiting = start_exchange(diag_tile, diag_rows, 0)
-    for copy in own[5:]:
+    clear()
+    for copy in own[4:]:
         copy.wait()
     for copy in beside:
         copy.wait_recv()
@@ -405,12 +442,7 @@
     finish_exchange(diag_waiting, diag_put, 0)
     remote.settle(diag_waiting)
 
-    def shift_diag(level, carry):
-        add = 4.0 + 2.0 * vertical[level] - middle
-        dd[level] = wide(double, (XR, XC)) * (dd[level] + add)
-        return carry
-
-    lax.fori_loop(0, 4, shift_diag, 0)
+    shift_diag()
 
     first_half = sub < 4
     lanes = iota((32, 128), 1)
@@ -431,16 +463,16 @@
                 if m == 0:
                     circle[2 * pp + n, 72:80, :] = pair[n]
         start = 8 + lax.rem(64 - shifts[j], 32)
-        kind = classes[j]
+        weight = [band[t, classes[j]] for t in range(4)]
         outs = []
         for n in range(2):
             now = circle[2 * pp + n, pl.ds(start, 32), :]
             before = circle[2 * pp + n, pl.ds(start - 1, 32), :]
             after = circle[2 * pp + n, pl.ds(start + 1, 32), :]
-            total = band[kind, 0] * pltpu.roll(jnp.where(lanes == 127, before, now), 1, 1)
-            total = total + band[kind, 1] * now
-            total = total + band[kind, 2] * pltpu.roll(jnp.where(lanes == 0, after, now), 127, 1)
-            total = total + band[kind, 3] * pltpu.roll(jnp.where(lanes < 2, after, now), 126, 1)
+            total = weight[0] * pltpu.roll(jnp.where(lanes == 127, before, now), 1, 1)
+            total = total + weight[1] * now
+            total = total + weight[2] * pltpu.roll(jnp.where(lanes == 0, after, now), 127, 1)
+            total = total + weight[3] * pltpu.roll(jnp.where(lanes < 2, after, now), 126, 1)
             outs.append(total)
         for m in range(4):
             a, b = outs[0][8 * m : 8 * m + 8], outs[1][8 * m : 8 * m + 8]
@@ -474,7 +506,6 @@
     back_edge = send_banded(64, 32)
     for copy in back_middle + back_edge:
         copy.wait_recv()
-    b_tile, b_rows, b_put = vector(0)
     for level in range(4):
         for b in range(4):
             place = 4 * level + b
@@ -493,21 +524,21 @@
         chebyshev(k - 1, None if k == 1 else k - 2, k)
     answer, worst = coefficients(gram(), STEPS, middle, half)
     combine(answer)
-    flag[...] = worst
+    flag[0, 0] = jnp.max(worst)
     remote.drain()
 
 
 def solve(source_field, helm_diag, vertical, band, offsets, shifts, classes, nlon, nlat):
-    copies = 2 + 4 * (nlon - 1) + 2 * 8 + (nlon - 1 + nlat - 1)
+    copies = 2 + 4 * (nlon - 1) + 2 * 8 + 15 + 7
     vmem = pl.BlockSpec(memory_space=pltpu.VMEM)
     smem = pl.BlockSpec(memory_space=pltpu.SMEM)
-    anywhere = pl.BlockSpec(memory_space=pl.ANY)
+    far = pl.BlockSpec(memory_space=pltpu.HBM)
     field = jax.ShapeDtypeStruct(source_field.shape, F32)
     return pl.pallas_call(
         partial(solve_kernel, nlon, nlat),
-        out_shape=(field, field, jax.ShapeDtypeStruct((8, 128), F32)),
-        in_specs=[smem] * 5 + [anywhere, anywhere],
-        out_specs=(vmem, vmem, vmem),
+        out_shape=(field, field, jax.ShapeDtypeStruct((1, 1), F32)),
+        in_specs=[smem] * 5 + [far, far],
+        out_specs=(vmem, vmem, smem),
         scratch_shapes=[
             pltpu.VMEM((4, 4, ROWS, 128), F32),
             pltpu.VMEM((4, 4, 3 * DRIFT, 128), F32),
@@ -517,14 +548,14 @@
             pltpu.VMEM((24, 80, 128), F32),
             pltpu.VMEM((nlon, 96, 128), F32),
             pltpu.VMEM((nlon * 96, 128), F32),
-            pltpu.VMEM((STEPS + 1, 6, XR, XC), F32),
-            pltpu.VMEM((4, XR, XC), F32),
+            pltpu.VMEM((STEPS + 1, 6, TILES, XR, 128), F32),
+            pltpu.VMEM((4, TILES, XR, 128), F32),
             pltpu.VMEM((2, 6, 2, 8, 128), F32),
             pltpu.VMEM((2, 2, 2, 8, 128), F32),
             pltpu.VMEM((128, 128), F32),
-            pltpu.VMEM((nlon, 8, 128), F32),
-            pltpu.VMEM((nlat, 8, 128), F32),
-            pltpu.SemaphoreType.DMA((13,)),
+            pltpu.VMEM((16, 8, 128), F32),
+            pltpu.VMEM((8, 8, 128), F32),
+            pltpu.SemaphoreType.DMA((16,)),
             pltpu.SemaphoreType.DMA((copies,)),
             pltpu.SemaphoreType.DMA((copies,)),
         ],
@@ -553,7 +584,7 @@
 
 def body(source_field, helm_diag, vertical, cubic_band, lat_offset, zonal_shift, row_class):
     departure, quick, worst = solve(
-        source_field, helm_diag, vertical, cubic_band, lat_offset, zonal_shift, row_class,
+        source_field, helm_diag, vertical, cubic_band.T, lat_offset, zonal_shift, row_class,
         lax.axis_size("lon"), lax.axis_size("lat"),
     )
     answer = lax.cond(

time: 52.6 us -> 66 us (1.25)
  Pallas kernels: 47.3 us -> 60 us
  local copies, waits for them, and re-layouts: 3.8 us -> 4.47 us
    pallas_call x1, Pallas kernels: 47.3 us -> 60 us  [solve(): pl.pallas_call(partial(solve_kernel, nlon, nlat), out_shape=(field, field...]
    unnamed x15 -> x16, local copies, waits for them, and re-layouts: 3.28 us -> 4.47 us
where the time goes in v4:
time: 66 us; the launch traced here: 65.8 us
  Pallas kernels  60 us (91%)
  local copies, waits for them, and re-layouts  4.47 us (7%)
  between operations  1.32 us (2%)
    pallas_call x1, Pallas kernels, solve(): pl.pallas_call(partial(solve_kernel, nlon, nlat), out_shape=(field, field...  60 us
    unnamed x16, local copies, waits for them, and re-layouts  4.47 us

profile of v4, /device:TPU:1, one launch (start us, length us, event | category | flops | bytes accessed | tf_op | source)
XLA Modules:
  0.0 65.8 jit_solution(17003593846662075666)
XLA Ops:
  0.6 0.0 copy-start.2
  0.6 0.0 copy-start.3
  0.7 0.0 copy-start.4
  0.7 0.6 copy-done.2
  1.3 0.0 copy-done.3
  1.3 0.0 copy-done.4
  1.3 0.0 copy-start
  1.3 1.0 %copy-done = f32[4,48,512]{2,1,0:T(8,128)S(1)} copy-done((f32[4,48,512]{2,1,0:T(8,128)S(1)}, f32[4,48,512]{2,1,0:T(8,128)}, u32[]{:S(2)}) %copy-start) | copy-done | bytes 393240
  2.3 0.0 copy-start.1
  2.3 0.7 %copy-done.1 = f32[8,4]{0,1:T(4,128)S(1)} copy-done((f32[8,4]{0,1:T(4,128)S(1)}, f32[8,4]{0,1:T(4,128)}, u32[]{:S(2)}) %copy-start.1) | copy-done | bytes 152
  3.0 0.0 copy-start.5
  3.0 60.0 %solve.1 = (f32[4,48,512]{2,1,0:T(8,128)S(1)}, f32[4,48,512]{2,1,0:T(8,128)S(1)}, f32[1,1]{1,0:T(1,128)}) custom-call(f32[4]{0:T(128)} %vertical.1, f32[4,8]{1,0:T(4,128)S(1)} %bitcast.2, s32[48]{0:T(128)S(1)} %copy-done.2, s32[48]{0:T(128)S(1)} %copy-done.3, s32[48]{0:T(128)S(1)} %copy-done.4, f32[4,48,512]{2,1,0:T(8,128)S(1)} %copy-done, f32[4,48,512]{2,1,0:T(8,128)} %helm.1), custom_call_target="tpu_custom_call" | custom-call | tf_op jit(solution)/shard_map/solve/pallas_call | solution.py:537
  63.6 0.0 copy-start.6
  63.6 0.0 copy-done.5
  63.6 0.6 copy-done.6
  64.3 0.7 %copy.28 = f32[4,48,512]{2,1,0:T(8,128)} copy(f32[4,48,512]{2,1,0:T(8,128)S(1)} %get-tuple-element.256) | data formatting | bytes 786432
  65.0 0.7 %copy.29 = f32[4,48,512]{2,1,0:T(8,128)} copy(f32[4,48,512]{2,1,0:T(8,128)S(1)} %get-tuple-element.258) | data formatting | bytes 786432
  (1 shorter events, 0.0 us)
Async XLA Ops:
  0.6 0.7 copy-start.2
  0.6 0.7 %copy-start.3 = (s32[48]{0:T(128)S(1)}, s32[48]{0:T(128)}, u32[]{:S(2)}) copy-start(s32[48]{0:T(128)} %shifts.1) | copy-start | bytes 580
  0.7 0.7 %copy-start.4 = (s32[48]{0:T(128)S(1)}, s32[48]{0:T(128)}, u32[]{:S(2)}) copy-start(s32[48]{0:T(128)} %classes.1) | copy-start | bytes 580
  1.3 1.0 %copy-start = (f32[4,48,512]{2,1,0:T(8,128)S(1)}, f32[4,48,512]{2,1,0:T(8,128)}, u32[]{:S(2)}) copy-start(f32[4,48,512]{2,1,0:T(8,128)} %source.1) | copy-start | bytes 1179652
  2.3 0.7 %copy-start.1 = (f32[8,4]{0,1:T(4,128)S(1)}, f32[8,4]{0,1:T(4,128)}, u32[]{:S(2)}) copy-start(f32[8,4]{0,1:T(4,128)} %param.14) | copy-start | bytes 388
  3.0 60.6 %copy-start.5 = (f32[4,48,512]{2,1,0:T(8,128)S(1)}, f32[4,48,512]{2,1,0:T(8,128)}, u32[]{:S(2)}) copy-start(f32[4,48,512]{2,1,0:T(8,128)} %helm.1) | copy-start | bytes 1179652
  63.6 0.7 %copy-start.6 = (f32[4]{0:T(128)S(1)}, f32[4]{0:T(128)}, u32[]{:S(2)}) copy-start(f32[4]{0:T(128)} %vertical.1) | copy-start | bytes 52

commit v5 on v4

--- a/solution.py
+++ b/solution.py
@@ -304,35 +304,42 @@
 
     def chebyshev(src, before, dst):
         last = dst == STEPS
-        first, count = (TOP, 3) if last else (TOP - 8, 4)
-
-        def one(i, carry):
-            level, pair = i // count, lax.rem(i, count)
-            for u in range(2):
-                r = pl.multiple_of(first + 16 * pair + 8 * u, 8)
+
+        def one(level, carry):
+            results = []
+            tiles = range(0, 6) if last else range(-1, 7)
+            at = lambda j, l, t, b: vs[j, l, b, TOP + 8 * t : TOP + 8 * t + 8, :]
+            for t in tiles:
                 scale = double
-                if not last and u == 0:
-                    scale = jnp.where(jnp.logical_or(pair > 0, top_ok), double, 0.0)
-                if not last and u == 1:
-                    scale = jnp.where(jnp.logical_or(pair < count - 1, bottom_ok), double, 0.0)
-                mids = [vs[src, level + 1, b, pl.ds(r, 8), :] for b in range(TILES)]
+                if t == -1:
+                    scale = jnp.where(top_ok, double, 0.0)
+                if t == 6:
+                    scale = jnp.where(bottom_ok, double, 0.0)
+                mids = [at(src, level + 1, t, b) for b in range(TILES)]
                 for b in range(4 if last else TILES):
                     mid = mids[b]
                     sides = pltpu.roll(jnp.where(lane == 127, mids[b - 1], mid), 1, 1)
                     sides = sides + pltpu.roll(jnp.where(lane == 0, mids[(b + 1) % TILES], mid), 127, 1)
-                    sides = sides + (
-                        vs[src, level + 1, b, pl.ds(r - 1, 8), :] + vs[src, level + 1, b, pl.ds(r + 1, 8), :]
-                    )
-                    stack = vs[src, level, b, pl.ds(r, 8), :] + vs[src, level + 2, b, pl.ds(r, 8), :]
-                    value = dd[level, b, pl.ds(r, 8), :] * mid - scale * (sides + vertical[level] * stack)
+                    above, below = at(src, level + 1, t - 1, b), at(src, level + 1, t + 1, b)
+                    sides = sides + pltpu.roll(jnp.where(sub == 7, above, mid), 1, 0)
+                    sides = sides + pltpu.roll(jnp.where(sub == 0, below, mid), 7, 0)
+                    stack = at(src, level, t, b) + at(src, level + 2, t, b)
+                    value = dd[level, b, TOP + 8 * t : TOP + 8 * t + 8, :] * mid - scale * (sides + vertical[level] * stack)
                     if before is None:
                         value = 0.5 * value
                     else:
-                        value = value - vs[before, level + 1, b, pl.ds(r, 8), :]
-                    vs[dst, level + 1, b, pl.ds(r, 8), :] = value
+                        value = value - at(before, level + 1, t, b)
+                    results.append((b, t, value))
+                    if len(results) == 20:
+                        for bb, tt, v in results:
+                            vs[dst, level + 1, bb, TOP + 8 * tt : TOP + 8 * tt + 8, :] = v
+                        results = []
+            for bb, tt, v in results:
+                vs[dst, level + 1, bb, TOP + 8 * tt : TOP + 8 * tt + 8, :] = v
             return carry
 
-        lax.fori_loop(0, 4 * count, one, 0)
+        for level in range(4):
+            one(level, 0)
 
     def all_reduce(value):
         for axes, slot in ((PLANE, slot_plane), (REST, slot_rest)):
@@ -353,7 +360,7 @@
         pairs = [(i, j) for i in range(count) for j in range(i, count) if i < STEPS]
 
         def one(t, sums):
-            level, r = t // 6, pl.multiple_of((t % 6) * 8, 8)
+            level, r = t // 6, (t % 6) * 8
             sums = list(sums)
             for b in range(4):
                 tiles = [vs[i, level + 1, b, pl.ds(r + TOP, 8), :] for i in range(count)]
@@ -361,7 +368,9 @@
                     sums[n] = sums[n] + tiles[i] * tiles[j]
             return tuple(sums)
 
-        sums = lax.fori_loop(0, 24, one, tuple(jnp.zeros((8, 128), F32) for _ in pairs))
+        sums = tuple(jnp.zeros((8, 128), F32) for _ in pairs)
+        for t in range(24):
+            sums = one(t, sums)
         for n, part in enumerate(sums):
             stage[n : n + 1, :] = jnp.sum(part, axis=0, keepdims=True)
         row = lax.dot_general(
@@ -372,7 +381,7 @@
 
     def combine(coef):
         def one(t, carry):
-            level, r = t // 6, pl.multiple_of((t % 6) * 8, 8)
+            level, r = t // 6, (t % 6) * 8
             for b in range(4):
                 value = None
                 for i, x in coef.items():
@@ -381,7 +390,8 @@
                 out[level, pl.ds(r, 8), 128 * b : 128 * b + 128] = value
             return carry
 
-        lax.fori_loop(0, 24, one, 0)
+        for t in range(24):
+            one(t, 0)
 
     for copy in own[0:4]:
         copy.wait()
@@ -560,7 +570,7 @@
             pltpu.SemaphoreType.DMA((copies,)),
         ],
         compiler_params=pltpu.CompilerParams(
-            collective_id=0, has_side_effects=True, vmem_limit_bytes=40 * 1024 * 1024
+            collective_id=0, has_side_effects=True, vmem_limit_bytes=62 * 1024 * 1024
         ),
         name="solve",
     )(vertical, band, offsets, shifts, classes, source_field, helm_diag)

time: 66 us -> 48 us (0.73)
  Pallas kernels: 60 us -> 44.1 us
  local copies, waits for them, and re-layouts: 4.47 us -> 2.15 us
    pallas_call x1, Pallas kernels: 60 us -> 44.1 us  [solve(): pl.pallas_call(partial(solve_kernel, nlon, nlat), out_shape=(field, field...]
    unnamed x16 -> x6, local copies, waits for them, and re-layouts: 4.47 us -> 2.15 us
where the time goes in v5:
time: 48 us; the launch traced here: 47.8 us
  Pallas kernels  44.1 us (92%)
  local copies, waits for them, and re-layouts  2.15 us (4%)
  between operations  1.36 us (3%)
    pallas_call x1, Pallas kernels, solve(): pl.pallas_call(partial(solve_kernel, nlon, nlat), out_shape=(field, field...  44.1 us
    unnamed x6, local copies, waits for them, and re-layouts  2.15 us

profile of v5, /device:TPU:1, one launch (start us, length us, event | category | flops | bytes accessed | tf_op | source)
XLA Modules:
  0.0 47.8 jit_solution(16354731636811651442)
XLA Ops:
  0.6 0.0 copy-start.1
  0.6 0.6 %copy-done.1 = f32[4]{0:T(128)S(1)} copy-done((f32[4]{0:T(128)S(1)}, f32[4]{0:T(128)}, u32[]{:S(2)}) %copy-start.1) | copy-done | bytes 40
  1.3 0.0 copy-start
  1.3 44.1 %solve.1 = (f32[4,48,512]{2,1,0:T(8,128)S(1)}, f32[4,48,512]{2,1,0:T(8,128)S(1)}, f32[1,1]{1,0:T(1,128)}) custom-call(f32[4]{0:T(128)S(1)} %copy-done.1, f32[4,8]{1,0:T(4,128)} %bitcast.2, s32[48]{0:T(128)} %offsets.1, s32[48]{0:T(128)} %shifts.1, s32[48]{0:T(128)} %classes.1, f32[4,48,512]{2,1,0:T(8,128)} %source.1, f32[4,48,512]{2,1,0:T(8,128)} %helm.1), custom_call_target="tpu_custom_call" | custom-call | tf_op jit(solution)/shard_map/solve/pallas_call | solution.py:547
  46.0 0.0 copy-done
  46.1 0.2 conditional.1
  46.3 0.7 %copy.28 = f32[4,48,512]{2,1,0:T(8,128)} copy(f32[4,48,512]{2,1,0:T(8,128)S(1)} %get-tuple-element.256) | data formatting | bytes 786432
  47.0 0.7 %copy.29 = f32[4,48,512]{2,1,0:T(8,128)} copy(f32[4,48,512]{2,1,0:T(8,128)S(1)} %get-tuple-element.258) | data formatting | bytes 786432
Async XLA Ops:
  0.6 0.7 %copy-start.1 = (f32[4]{0:T(128)S(1)}, f32[4]{0:T(128)}, u32[]{:S(2)}) copy-start(f32[4]{0:T(128)} %vertical.1) | copy-start | bytes 52
  1.3 44.8 %copy-start = (f32[4,48,512]{2,1,0:T(8,128)S(1)}, f32[4,48,512]{2,1,0:T(8,128)}, u32[]{:S(2)}) copy-start(f32[4,48,512]{2,1,0:T(8,128)} %helm.1) | copy-start | bytes 1179652

commit v6 on v5

--- a/solution.py
+++ b/solution.py
@@ -55,6 +55,8 @@
 STEPS = 8
 SIZES = {"zl": 2, "x": 4, "zh": 2, "y": 4, "c": 2}
 PLANE, REST = ("x", "y"), ("zl", "zh", "c")
+PART = 120
+FAR_FIRST = [6, 2, 5, 7, 3, 1, 4]
 LIMIT = 1.5e4
 ROWS, COLS = 48, 512
 XR, TOP, TILES = 80, 16, 5
@@ -155,7 +157,7 @@
 
 def solve_kernel(
     nlon, nlat, vertical, band, offsets, shifts, classes, source, helm, dep, out, flag,
-    inner, upper, lower, picked, gathered, circle, banded, returned,
+    inner, upper, lower, picked, gathered, circle, looped, banded, returned, beyond,
     vs, dd, lon_in, packs, stage, slot_plane, slot_rest, local_sems, send_sems, recv_sems,
 ):
     lon, lat = lax.axis_index("lon"), lax.axis_index("lat")
@@ -179,8 +181,7 @@
 
     barrier = pltpu.get_barrier_semaphore()
     greet = [(east(k), lat) for k in range(1, nlon)]
-    greet += [(lon, north(1)), (lon, north(-1))]
-    greet += [(east(a), north(b)) for a in (-1, 1) for b in (-1, 1)]
+    greet += [(east(k), north(b)) for k in range(nlon) for b in (-1, 1)]
     greet += [place_of(m) for m in partners(PLANE) if m["y"]]
     greet += [place_of(m) for m in partners(REST) if m["zh"] or m["c"]]
     for peer in greet:
@@ -271,14 +272,8 @@
                     for b in range(5):
                         put(level, t, b, jnp.zeros((8, 128), F32))
 
-    def b_tile(level, t, b):
-        return vs[0, level + 1, b, TOP + 8 * t : TOP + 8 * t + 8, :]
-
     def b_put(level, t, b, value):
         vs[0, level + 1, b, TOP + 8 * t : TOP + 8 * t + 8, :] = value
-
-    def b_rows(at):
-        return vs.at[0, pl.ds(1, 4), pl.ds(0, 4), pl.ds(at, 8), :]
 
     def diag_tile(level, t, b):
         return dd[level, b, TOP + 8 * t : TOP + 8 * t + 8, :]
@@ -457,10 +452,9 @@
     first_half = sub < 4
     lanes = iota((32, 128), 1)
 
-    def band_rows(pp, j):
-        low = pl.multiple_of(pp * 8, 8)
+    def fill_circle(pp):
         for m in range(4):
-            a, b = gathered[2 * m, pl.ds(low, 8), :], gathered[2 * m + 1, pl.ds(low, 8), :]
+            a, b = gathered[2 * m, 8 * pp : 8 * pp + 8, :], gathered[2 * m + 1, 8 * pp : 8 * pp + 8, :]
             pair = (
                 jnp.where(first_half, a, pltpu.roll(b, 4, 0)),
                 jnp.where(first_half, pltpu.roll(a, 4, 0), b),
@@ -472,64 +466,104 @@
                     circle[2 * pp + n, 0:8, :] = pair[n]
                 if m == 0:
                     circle[2 * pp + n, 72:80, :] = pair[n]
+
+    def band_row(row, j, at, edge_at):
         start = 8 + lax.rem(64 - shifts[j], 32)
         weight = [band[t, classes[j]] for t in range(4)]
         outs = []
-        for n in range(2):
-            now = circle[2 * pp + n, pl.ds(start, 32), :]
-            before = circle[2 * pp + n, pl.ds(start - 1, 32), :]
-            after = circle[2 * pp + n, pl.ds(start + 1, 32), :]
+        for level in range(4):
+            now = circle[4 * row + level, pl.ds(start, 32), :]
+            before = circle[4 * row + level, pl.ds(start - 1, 32), :]
+            after = circle[4 * row + level, pl.ds(start + 1, 32), :]
             total = weight[0] * pltpu.roll(jnp.where(lanes == 127, before, now), 1, 1)
             total = total + weight[1] * now
             total = total + weight[2] * pltpu.roll(jnp.where(lanes == 0, after, now), 127, 1)
             total = total + weight[3] * pltpu.roll(jnp.where(lanes < 2, after, now), 126, 1)
             outs.append(total)
-        for m in range(4):
-            a, b = outs[0][8 * m : 8 * m + 8], outs[1][8 * m : 8 * m + 8]
-            banded[2 * m, pl.ds(low, 8), :] = jnp.where(first_half, a, pltpu.roll(b, 4, 0))
-            banded[2 * m + 1, pl.ds(low, 8), :] = jnp.where(first_half, pltpu.roll(a, 4, 0), b)
-
-    def middle_band(pp, carry):
-        band_rows(pp, DRIFT + 4 * lon + pp // 2)
-        return carry
-
-    def edge_band(pp, carry):
-        band_rows(pp, lon + (ROWS - DRIFT) * ((pp - 8) // 2))
-        return carry
+        for half in range(2):
+            for m in range(4):
+                a, b = outs[2 * half][8 * m : 8 * m + 8], outs[2 * half + 1][8 * m : 8 * m + 8]
+                here = slice(at + 8 * half, at + 8 * half + 8)
+                banded[2 * m, here, :] = jnp.where(first_half, a, pltpu.roll(b, 4, 0))
+                banded[2 * m + 1, here, :] = jnp.where(first_half, pltpu.roll(a, 4, 0), b)
+        edges = jnp.zeros((8, 128), F32)
+        for level in range(4):
+            looped[4 * row + level, 0:8, :] = outs[level][24:32]
+            looped[4 * row + level, 8:40, :] = outs[level]
+            looped[4 * row + level, 40:48, :] = outs[level][0:8]
+        for level in range(4):
+            west = looped[4 * row + level, pl.ds(7, 8, stride=4), :]
+            east_ = looped[4 * row + level, pl.ds(12, 8, stride=4), :]
+            both = pltpu.roll(jnp.where(lane < 64, east_, west), 16 * level + 8, 1)
+            edges = jnp.where(lane // 16 == level, both, edges)
+        for d in range(nlon):
+            banded[d, edge_at : edge_at + 1, :] = edges[d : d + 1]
 
     def send_banded(start, size):
-        here = pl.multiple_of(lon * 96 + start, 8)
+        here = pl.multiple_of(lon * PART + start, 8)
         copies = [
             remote.start(banded.at[east(k), pl.ds(start, size)], returned.at[pl.ds(here, size)], east(k), lat)
-            for k in range(1, nlon)
+            for k in FAR_FIRST
         ]
         returned[pl.ds(here, size), :] = banded[lon, pl.ds(start, size), :]
         return copies
 
+    def send_beyond():
+        here = pl.multiple_of(lon * 24, 8)
+        copies = []
+        for k in FAR_FIRST + [0]:
+            for start, side, step in ((96, 0, 1), (72, 1, -1)):
+                copies.append(
+                    remote.start(
+                        banded.at[east(k), pl.ds(start, 24)], beyond.at[side, pl.ds(here, 24)], east(k), north(step)
+                    )
+                )
+        return copies
+
     for copy in sent_middle:
         copy.wait_recv()
-    lax.fori_loop(0, 8, middle_band, 0)
-    back_middle = send_banded(0, 64)
+    for pp in range(8):
+        fill_circle(pp)
+    for q in range(4):
+        band_row(q, DRIFT + 4 * lon + q, 16 * q, 64 + q)
+    arriving = send_banded(0, 72)
     for copy in sent_edge:
         copy.wait_recv()
-    lax.fori_loop(8, 12, edge_band, 0)
-    back_edge = send_banded(64, 32)
-    for copy in back_middle + back_edge:
+    for pp in range(8, 12):
+        fill_circle(pp)
+    band_row(4, lon, 72, 88)
+    band_row(5, lon + ROWS - DRIFT, 96, 112)
+    arriving += send_beyond() + send_banded(72, 48)
+    for copy in arriving:
         copy.wait_recv()
-    for level in range(4):
-        for b in range(4):
-            place = 4 * level + b
-            for t in range(6):
-                if t in (0, 5):
-                    tile = returned[pl.ds(64 + 16 * (t // 5) + place, 8, stride=96), :]
-                else:
-                    tile = jnp.concatenate(
-                        [returned[pl.ds((2 * t - 2 + n) * 96 + place, 4, stride=16), :] for n in range(2)], 0
-                    )
+
+    def row_tile(t, place, beside):
+        if t in (-1, 6):
+            place = 16 if beside else place
+            return beyond[t // 6 if t > 0 else 0, pl.ds(place, 8, stride=24), :]
+        if t in (0, 5):
+            place = 16 if beside else place
+            return returned[pl.ds(72 + 24 * (t // 5) + place, 8, stride=PART), :]
+        both = []
+        for c in (2 * t - 2, 2 * t - 1):
+            if beside:
+                both.append(returned[c * PART + 64 : c * PART + 68, :])
+            else:
+                both.append(returned[pl.ds(c * PART + place, 4, stride=16), :])
+        return jnp.concatenate(both, 0)
+
+    for t in range(-1, 7):
+        outside = {-1: top_ok, 6: bottom_ok}.get(t)
+        beside = row_tile(t, 0, True)
+        for level in range(4):
+            tiles = [row_tile(t, 4 * level + b, False) for b in range(4)]
+            tiles.append(pltpu.roll(beside, (120 - 16 * level) % 128, 1))
+            for b, tile in enumerate(tiles):
+                if outside is not None:
+                    tile = jnp.where(outside, tile, 0.0)
+                elif b < 4:
+                    dep[level, 8 * t : 8 * t + 8, 128 * b : 128 * b + 128] = tile
                 b_put(level, t, b, tile)
-                dep[level, 8 * t : 8 * t + 8, 128 * b : 128 * b + 128] = tile
-    waiting = start_exchange(b_tile, b_rows, 1)
-    finish_exchange(waiting, b_put, 1)
     for k in range(1, STEPS + 1):
         chebyshev(k - 1, None if k == 1 else k - 2, k)
     answer, worst = coefficients(gram(), STEPS, middle, half)
@@ -539,7 +573,7 @@
 
 
 def solve(source_field, helm_diag, vertical, band, offsets, shifts, classes, nlon, nlat):
-    copies = 2 + 4 * (nlon - 1) + 2 * 8 + 15 + 7
+    copies = 2 + 4 * (nlon - 1) + 8 + 2 * nlon + 15 + 7
     vmem = pl.BlockSpec(memory_space=pltpu.VMEM)
     smem = pl.BlockSpec(memory_space=pltpu.SMEM)
     far = pl.BlockSpec(memory_space=pltpu.HBM)
@@ -556,12 +590,14 @@
             pltpu.VMEM((nlon - 1, 96, 128), F32),
             pltpu.VMEM((nlon, 96, 128), F32),
             pltpu.VMEM((24, 80, 128), F32),
-            pltpu.VMEM((nlon, 96, 128), F32),
-            pltpu.VMEM((nlon * 96, 128), F32),
+            pltpu.VMEM((24, 48, 128), F32),
+            pltpu.VMEM((nlon, PART, 128), F32),
+            pltpu.VMEM((nlon * PART, 128), F32),
+            pltpu.VMEM((2, nlon * 24, 128), F32),
             pltpu.VMEM((STEPS + 1, 6, TILES, XR, 128), F32),
             pltpu.VMEM((4, TILES, XR, 128), F32),
-            pltpu.VMEM((2, 6, 2, 8, 128), F32),
-            pltpu.VMEM((2, 2, 2, 8, 128), F32),
+            pltpu.VMEM((1, 6, 2, 8, 128), F32),
+            pltpu.VMEM((1, 2, 2, 8, 128), F32),
             pltpu.VMEM((128, 128), F32),
             pltpu.VMEM((16, 8, 128), F32),
             pltpu.VMEM((8, 8, 128), F32),

time: 48 us -> 46.9 us (0.977)
  Pallas kernels: 44.1 us -> 43 us
    pallas_call x1, Pallas kernels: 44.1 us -> 43 us  [solve(): pl.pallas_call(partial(solve_kernel, nlon, nlat), out_shape=(field, field...]
where the time goes in v6:
time: 46.9 us; the launch traced here: 46.8 us
  Pallas kernels  43 us (92%)
  local copies, waits for them, and re-layouts  2.15 us (5%)
  between operations  1.36 us (3%)
    pallas_call x1, Pallas kernels, solve(): pl.pallas_call(partial(solve_kernel, nlon, nlat), out_shape=(field, field...  43 us
    unnamed x6, local copies, waits for them, and re-layouts  2.15 us

profile of v6, /device:TPU:1, one launch (start us, length us, event | category | flops | bytes accessed | tf_op | source)
XLA Modules:
  0.0 46.8 jit_solution(17557702356278073818)
XLA Ops:
  0.6 0.0 copy-start.1
  0.6 0.6 %copy-done.1 = f32[4]{0:T(128)S(1)} copy-done((f32[4]{0:T(128)S(1)}, f32[4]{0:T(128)}, u32[]{:S(2)}) %copy-start.1) | copy-done | bytes 40
  1.3 0.0 copy-start
  1.3 43.0 %solve.1 = (f32[4,48,512]{2,1,0:T(8,128)S(1)}, f32[4,48,512]{2,1,0:T(8,128)S(1)}, f32[1,1]{1,0:T(1,128)}) custom-call(f32[4]{0:T(128)S(1)} %copy-done.1, f32[4,8]{1,0:T(4,128)} %bitcast.2, s32[48]{0:T(128)} %offsets.1, s32[48]{0:T(128)} %shifts.1, s32[48]{0:T(128)} %classes.1, f32[4,48,512]{2,1,0:T(8,128)} %source.1, f32[4,48,512]{2,1,0:T(8,128)} %helm.1), custom_call_target="tpu_custom_call" | custom-call | tf_op jit(solution)/shard_map/solve/pallas_call | solution.py:581
  45.0 0.0 copy-done
  45.0 0.2 conditional.1
  45.3 0.7 %copy.28 = f32[4,48,512]{2,1,0:T(8,128)} copy(f32[4,48,512]{2,1,0:T(8,128)S(1)} %get-tuple-element.256) | data formatting | bytes 786432
  46.0 0.7 %copy.29 = f32[4,48,512]{2,1,0:T(8,128)} copy(f32[4,48,512]{2,1,0:T(8,128)S(1)} %get-tuple-element.258) | data formatting | bytes 786432
Async XLA Ops:
  0.6 0.7 %copy-start.1 = (f32[4]{0:T(128)S(1)}, f32[4]{0:T(128)}, u32[]{:S(2)}) copy-start(f32[4]{0:T(128)} %vertical.1) | copy-start | bytes 52
  1.3 43.7 %copy-start = (f32[4,48,512]{2,1,0:T(8,128)S(1)}, f32[4,48,512]{2,1,0:T(8,128)}, u32[]{:S(2)}) copy-start(f32[4,48,512]{2,1,0:T(8,128)} %helm.1) | copy-start | bytes 1179652

commit v7 on v6

--- a/solution.py
+++ b/solution.py
@@ -55,7 +55,7 @@
 STEPS = 8
 SIZES = {"zl": 2, "x": 4, "zh": 2, "y": 4, "c": 2}
 PLANE, REST = ("x", "y"), ("zl", "zh", "c")
-PART = 120
+PART = 112
 FAR_FIRST = [6, 2, 5, 7, 3, 1, 4]
 LIMIT = 1.5e4
 ROWS, COLS = 48, 512
@@ -156,7 +156,8 @@
 
 
 def solve_kernel(
-    nlon, nlat, vertical, band, offsets, shifts, classes, source, helm, dep, out, flag,
+    nlon, nlat, vertical_far, band_far, offsets_far, shifts_far, classes_far, source, helm, dep, out, flag,
+    vertical, band, offsets, shifts, classes,
     inner, upper, lower, picked, gathered, circle, looped, banded, returned, beyond,
     vs, dd, lon_in, packs, stage, slot_plane, slot_rest, local_sems, send_sems, recv_sems,
 ):
@@ -168,6 +169,17 @@
     def north(k):
         return lax.rem(lat + (k + nlat), nlat)
 
+    small = [
+        pltpu.make_async_copy(a, b, local_sems.at[16 + n])
+        for n, (a, b) in enumerate(
+            [
+                (vertical_far, vertical), (band_far, band), (offsets_far, offsets),
+                (shifts_far, shifts), (classes_far, classes),
+            ]
+        )
+    ]
+    for copy in small:
+        copy.start()
     here = {"zl": lon // 4, "x": lax.rem(lon, 4), "zh": lat // 8, "y": lax.rem(lat // 2, 4), "c": lax.rem(lat, 2)}
 
     def place_of(moves):
@@ -227,6 +239,8 @@
         lax.fori_loop(0, STEPS + 1, one, 0)
         stage[...] = jnp.zeros_like(stage)
 
+    for copy in small:
+        copy.wait()
     mean = 0.25 * ((vertical[0] + vertical[1]) + (vertical[2] + vertical[3]))
     top = 0.9 * (9.0 + 4.0 * mean)
     middle, half = 0.54 * top, 0.46 * top
@@ -341,7 +355,7 @@
             mine = 0
             for axis in axes:
                 mine = mine * SIZES[axis] + here[axis]
-            slot[mine] = value
+            slot[mine] = value[0:1]
             copies = [remote.start(slot.at[mine], slot.at[mine], *place_of(m)) for m in partners(axes)]
             for copy in copies:
                 copy.wait_recv()
@@ -512,10 +526,10 @@
         here = pl.multiple_of(lon * 24, 8)
         copies = []
         for k in FAR_FIRST + [0]:
-            for start, side, step in ((96, 0, 1), (72, 1, -1)):
+            for start, side, step in ((89, 0, 1), (72, 1, -1)):
                 copies.append(
                     remote.start(
-                        banded.at[east(k), pl.ds(start, 24)], beyond.at[side, pl.ds(here, 24)], east(k), north(step)
+                        banded.at[east(k), pl.ds(start, 17)], beyond.at[side, pl.ds(here, 17)], east(k), north(step)
                     )
                 )
         return copies
@@ -526,24 +540,24 @@
         fill_circle(pp)
     for q in range(4):
         band_row(q, DRIFT + 4 * lon + q, 16 * q, 64 + q)
-    arriving = send_banded(0, 72)
+    arriving = send_banded(0, 68)
     for copy in sent_edge:
         copy.wait_recv()
     for pp in range(8, 12):
         fill_circle(pp)
     band_row(4, lon, 72, 88)
-    band_row(5, lon + ROWS - DRIFT, 96, 112)
-    arriving += send_beyond() + send_banded(72, 48)
+    band_row(5, lon + ROWS - DRIFT, 90, 89)
+    arriving += send_beyond() + send_banded(72, 34)
     for copy in arriving:
         copy.wait_recv()
 
     def row_tile(t, place, beside):
         if t in (-1, 6):
-            place = 16 if beside else place
+            place = (16 if t > 0 else 0) if beside else place + (t < 0)
             return beyond[t // 6 if t > 0 else 0, pl.ds(place, 8, stride=24), :]
         if t in (0, 5):
-            place = 16 if beside else place
-            return returned[pl.ds(72 + 24 * (t // 5) + place, 8, stride=PART), :]
+            place = 88 + t // 5 if beside else 72 + 18 * (t // 5) + place
+            return returned[pl.ds(place, 8, stride=PART), :]
         both = []
         for c in (2 * t - 2, 2 * t - 1):
             if beside:
@@ -581,9 +595,14 @@
     return pl.pallas_call(
         partial(solve_kernel, nlon, nlat),
         out_shape=(field, field, jax.ShapeDtypeStruct((1, 1), F32)),
-        in_specs=[smem] * 5 + [far, far],
+        in_specs=[far] * 7,
         out_specs=(vmem, vmem, smem),
         scratch_shapes=[
+            pltpu.SMEM((4,), F32),
+            pltpu.SMEM(band.shape, F32),
+            pltpu.SMEM(offsets.shape, jnp.int32),
+            pltpu.SMEM(shifts.shape, jnp.int32),
+            pltpu.SMEM(classes.shape, jnp.int32),
             pltpu.VMEM((4, 4, ROWS, 128), F32),
             pltpu.VMEM((4, 4, 3 * DRIFT, 128), F32),
             pltpu.VMEM((4, 4, 3 * DRIFT, 128), F32),
@@ -599,9 +618,9 @@
             pltpu.VMEM((1, 6, 2, 8, 128), F32),
             pltpu.VMEM((1, 2, 2, 8, 128), F32),
             pltpu.VMEM((128, 128), F32),
-            pltpu.VMEM((16, 8, 128), F32),
-            pltpu.VMEM((8, 8, 128), F32),
-            pltpu.SemaphoreType.DMA((16,)),
+            pltpu.VMEM((16, 1, 128), F32),
+            pltpu.VMEM((8, 1, 128), F32),
+            pltpu.SemaphoreType.DMA((21,)),
             pltpu.SemaphoreType.DMA((copies,)),
             pltpu.SemaphoreType.DMA((copies,)),
         ],
@@ -610,6 +629,31 @@
         ),
         name="solve",
     )(vertical, band, offsets, shifts, classes, source_field, helm_diag)
+
+
+def finish_kernel(departure, answer, departure_out, answer_out, sems):
+    copies = [
+        pltpu.make_async_copy(a.at[k], b.at[k], sems.at[n, k])
+        for n, (a, b) in enumerate([(departure, departure_out), (answer, answer_out)])
+        for k in range(4)
+    ]
+    for copy in copies:
+        copy.start()
+    for copy in copies:
+        copy.wait()
+
+
+def finish(departure, answer):
+    anywhere = pl.BlockSpec(memory_space=pl.ANY)
+    field = jax.ShapeDtypeStruct(departure.shape, F32)
+    return pl.pallas_call(
+        finish_kernel,
+        out_shape=(field, field),
+        in_specs=[anywhere] * 2,
+        out_specs=(anywhere, anywhere),
+        scratch_shapes=[pltpu.SemaphoreType.DMA((2, 4))],
+        name="finish",
+    )(departure, answer)
 
 
 def iterate(departure, helm_diag, vertical):
@@ -636,7 +680,7 @@
     answer = lax.cond(
         worst[0, 0] < LIMIT, lambda *_: quick, iterate, departure, helm_diag, vertical
     )
-    return (departure, answer)
+    return finish(departure, answer)
 
 
 def solution(mesh):

time: 46.9 us -> 43.8 us (0.934)
  Pallas kernels: 43 us -> 41.2 us
  local copies, waits for them, and re-layouts: 2.15 us -> 0.65 us
    pallas_call x1, Pallas kernels: 43 us -> 40.2 us  [solve(): pl.pallas_call(partial(solve_kernel, nlon, nlat), out_shape=(field, field...]
    unnamed x6 -> x4, local copies, waits for them, and re-layouts: 2.15 us -> 0.65 us
    pallas_call x0 -> x1, Pallas kernels: none -> 0.94 us  [finish(): pl.pallas_call(finish_kernel, out_shape=(field, field), in_specs=[anywher...]
where the time goes in v7:
time: 43.8 us; the launch traced here: 43.6 us
  Pallas kernels  41.2 us (94%)
  between operations  1.54 us (4%)
  local copies, waits for them, and re-layouts  0.65 us (1%)
    pallas_call x1, Pallas kernels, solve(): pl.pallas_call(partial(solve_kernel, nlon, nlat), out_shape=(field, field...  40.2 us
    pallas_call x1, Pallas kernels, finish(): pl.pallas_call(finish_kernel, out_shape=(field, field), in_specs=[anywher...  0.94 us

profile of v7, /device:TPU:1, one launch (start us, length us, event | category | flops | bytes accessed | tf_op | source)
XLA Modules:
  0.0 43.6 jit_solution(16605444838556961320)
XLA Ops:
  0.6 0.0 copy-start.1
  0.6 0.6 %copy-done.1 = f32[4]{0:T(128)S(1)} copy-done((f32[4]{0:T(128)S(1)}, f32[4]{0:T(128)}, u32[]{:S(2)}) %copy-start.1) | copy-done | bytes 40
  1.3 0.0 copy-start
  1.3 40.2 %solve.1 = (f32[4,48,512]{2,1,0:T(8,128)S(1)}, f32[4,48,512]{2,1,0:T(8,128)S(1)}, f32[1,1]{1,0:T(1,128)}) custom-call(f32[4]{0:T(128)S(1)} %copy-done.1, f32[4,8]{1,0:T(4,128)} %bitcast.2, s32[48]{0:T(128)} %offsets_far.1, s32[48]{0:T(128)} %shifts_far.1, s32[48]{0:T(128)} %classes_far.1, f32[4,48,512]{2,1,0:T(8,128)} %source.1, f32[4,48,512]{2,1,0:T(8,128)} %helm.1), custom_call_target="tpu_custom_call" | custom-call | tf_op jit(solution)/shard_map/solve/pallas_call | solution.py:595
  42.2 0.0 copy-done
  42.2 0.2 conditional.1
  42.5 0.9 %finish.1 = (f32[4,48,512]{2,1,0:T(8,128)}, f32[4,48,512]{2,1,0:T(8,128)}) custom-call(f32[4,48,512]{2,1,0:T(8,128)S(1)} %get-tuple-element.109.departure, f32[4,48,512]{2,1,0:T(8,128)S(1)} %get-tuple-element.254.answer), custom_call_target="tpu_custom_call" | custom-call | tf_op jit(solution)/shard_map/finish/pallas_call | solution.py:649
Async XLA Ops:
  0.6 0.7 %copy-start.1 = (f32[4]{0:T(128)S(1)}, f32[4]{0:T(128)}, u32[]{:S(2)}) copy-start(f32[4]{0:T(128)} %vertical_far.1) | copy-start | bytes 52
  1.3 40.9 %copy-start = (f32[4,48,512]{2,1,0:T(8,128)S(1)}, f32[4,48,512]{2,1,0:T(8,128)}, u32[]{:S(2)}) copy-start(f32[4,48,512]{2,1,0:T(8,128)} %helm.1) | copy-start | bytes 1179652

commit v8 on v7

--- a/solution.py
+++ b/solution.py
@@ -156,7 +156,7 @@
 
 
 def solve_kernel(
-    nlon, nlat, vertical_far, band_far, offsets_far, shifts_far, classes_far, source, helm, dep, out, flag,
+    nlon, nlat, vertical_far, band_far, offsets_far, shifts_far, classes_far, source, helm, dep, out, flag, coupling,
     vertical, band, offsets, shifts, classes,
     inner, upper, lower, picked, gathered, circle, looped, banded, returned, beyond,
     vs, dd, lon_in, packs, stage, slot_plane, slot_rest, local_sems, send_sems, recv_sems,
@@ -583,6 +583,8 @@
     answer, worst = coefficients(gram(), STEPS, middle, half)
     combine(answer)
     flag[0, 0] = jnp.max(worst)
+    for k in range(4):
+        coupling[k : k + 1, :] = jnp.full((1, 128), vertical[k], F32)
     remote.drain()
 
 
@@ -594,9 +596,9 @@
     field = jax.ShapeDtypeStruct(source_field.shape, F32)
     return pl.pallas_call(
         partial(solve_kernel, nlon, nlat),
-        out_shape=(field, field, jax.ShapeDtypeStruct((1, 1), F32)),
+        out_shape=(pltpu.VMEM(field.shape, F32), pltpu.VMEM(field.shape, F32), pltpu.SMEM((1, 1), F32), pltpu.VMEM((4, 128), F32)),
         in_specs=[far] * 7,
-        out_specs=(vmem, vmem, smem),
+        out_specs=(vmem, vmem, smem, vmem),
         scratch_shapes=[
             pltpu.SMEM((4,), F32),
             pltpu.SMEM(band.shape, F32),
@@ -656,7 +658,9 @@
     )(departure, answer)
 
 
-def iterate(departure, helm_diag, vertical):
+def iterate(departure, helm_diag, coupling):
+    vertical = coupling[:, 0]
+
     def one(_, carry):
         answer, residual, direction, norm = carry
         applied = operate(direction, helm_diag, vertical)
@@ -673,12 +677,12 @@
 
 
 def body(source_field, helm_diag, vertical, cubic_band, lat_offset, zonal_shift, row_class):
-    departure, quick, worst = solve(
+    departure, quick, worst, coupling = solve(
         source_field, helm_diag, vertical, cubic_band.T, lat_offset, zonal_shift, row_class,
         lax.axis_size("lon"), lax.axis_size("lat"),
     )
     answer = lax.cond(
-        worst[0, 0] < LIMIT, lambda *_: quick, iterate, departure, helm_diag, vertical
+        worst[0, 0] < LIMIT, lambda *_: quick, iterate, departure, helm_diag, coupling
     )
     return finish(departure, answer)
 

time: 43.8 us -> 42.1 us (0.961)
  between operations: 1.54 us -> 0.85 us
  local copies, waits for them, and re-layouts: 0.65 us -> 0.01 us
    unnamed x4 -> x2, local copies, waits for them, and re-layouts: 0.65 us -> 0.01 us
where the time goes in v8:
time: 42.1 us; the launch traced here: 41.9 us
  Pallas kernels  40.8 us (97%)
  between operations  0.85 us (2%)
    pallas_call x1, Pallas kernels, solve(): pl.pallas_call(partial(solve_kernel, nlon, nlat), out_shape=(pltpu.VMEM(f...  39.9 us
    pallas_call x1, Pallas kernels, finish(): pl.pallas_call(finish_kernel, out_shape=(field, field), in_specs=[anywher...  0.94 us

profile of v8, /device:TPU:1, one launch (start us, length us, event | category | flops | bytes accessed | tf_op | source)
XLA Modules:
  0.0 41.9 jit_solution(11783934949455252732)
XLA Ops:
  0.6 0.0 copy-start
  0.6 39.9 %solve.1 = (f32[4,48,512]{2,1,0:T(8,128)S(1)}, f32[4,48,512]{2,1,0:T(8,128)S(1)}, f32[1,1]{1,0:T(1,128)S(4)}, f32[4,128]{1,0:T(4,128)S(1)}) custom-call(f32[4]{0:T(128)} %vertical_far.1, f32[4,8]{1,0:T(4,128)} %bitcast.12, s32[48]{0:T(128)} %offsets_far.1, s32[48]{0:T(128)} %shifts_far.1, s32[48]{0:T(128)} %classes_far.1, f32[4,48,512]{2,1,0:T(8,128)} %source.1, ...), custom_call_target="tpu_custom_call" | custom-call | tf_op jit(solution)/shard_map/solve/pallas_call | solution.py:597
  40.5 0.0 copy-done
  40.5 0.2 conditional.1
  40.8 0.9 %finish.1 = (f32[4,48,512]{2,1,0:T(8,128)}, f32[4,48,512]{2,1,0:T(8,128)}) custom-call(f32[4,48,512]{2,1,0:T(8,128)S(1)} %get-tuple-element.110.departure, f32[4,48,512]{2,1,0:T(8,128)S(1)} %get-tuple-element.261.answer), custom_call_target="tpu_custom_call" | custom-call | tf_op jit(solution)/shard_map/finish/pallas_call | solution.py:651
Async XLA Ops:
  0.6 39.9 %copy-start = (f32[4,48,512]{2,1,0:T(8,128)S(1)}, f32[4,48,512]{2,1,0:T(8,128)}, u32[]{:S(2)}) copy-start(f32[4,48,512]{2,1,0:T(8,128)} %helm.1) | copy-start | bytes 1179652

commit v9 on v8

--- a/solution.py
+++ b/solution.py
@@ -193,7 +193,7 @@
 
     barrier = pltpu.get_barrier_semaphore()
     greet = [(east(k), lat) for k in range(1, nlon)]
-    greet += [(east(k), north(b)) for k in range(nlon) for b in (-1, 1)]
+    greet += [(east(k), north(b)) for k in (-1, 0, 1) for b in (-1, 1)]
     greet += [place_of(m) for m in partners(PLANE) if m["y"]]
     greet += [place_of(m) for m in partners(REST) if m["zh"] or m["c"]]
     for peer in greet:

time: 42.1 us -> 42 us (level)
  no operation moved by 1% of the time
where the time goes in v9:
time: 42 us; the launch traced here: 41.8 us
  Pallas kernels  40.7 us (97%)
  between operations  0.85 us (2%)
    pallas_call x1, Pallas kernels, solve(): pl.pallas_call(partial(solve_kernel, nlon, nlat), out_shape=(pltpu.VMEM(f...  39.8 us
    pallas_call x1, Pallas kernels, finish(): pl.pallas_call(finish_kernel, out_shape=(field, field), in_specs=[anywher...  0.94 us

profile of v9, /device:TPU:1, one launch (start us, length us, event | category | flops | bytes accessed | tf_op | source)
XLA Modules:
  0.0 41.8 jit_solution(8952632908699907881)
XLA Ops:
  0.6 0.0 copy-start
  0.6 39.8 %solve.1 = (f32[4,48,512]{2,1,0:T(8,128)S(1)}, f32[4,48,512]{2,1,0:T(8,128)S(1)}, f32[1,1]{1,0:T(1,128)S(4)}, f32[4,128]{1,0:T(4,128)S(1)}) custom-call(f32[4]{0:T(128)} %vertical_far.1, f32[4,8]{1,0:T(4,128)} %bitcast.12, s32[48]{0:T(128)} %offsets_far.1, s32[48]{0:T(128)} %shifts_far.1, s32[48]{0:T(128)} %classes_far.1, f32[4,48,512]{2,1,0:T(8,128)} %source.1, ...), custom_call_target="tpu_custom_call" | custom-call | tf_op jit(solution)/shard_map/solve/pallas_call | solution.py:597
  40.5 0.0 copy-done
  40.5 0.2 conditional.1
  40.7 0.9 %finish.1 = (f32[4,48,512]{2,1,0:T(8,128)}, f32[4,48,512]{2,1,0:T(8,128)}) custom-call(f32[4,48,512]{2,1,0:T(8,128)S(1)} %get-tuple-element.110.departure, f32[4,48,512]{2,1,0:T(8,128)S(1)} %get-tuple-element.261.answer), custom_call_target="tpu_custom_call" | custom-call | tf_op jit(solution)/shard_map/finish/pallas_call | solution.py:651
Async XLA Ops:
  0.6 39.8 %copy-start = (f32[4,48,512]{2,1,0:T(8,128)S(1)}, f32[4,48,512]{2,1,0:T(8,128)}, u32[]{:S(2)}) copy-start(f32[4,48,512]{2,1,0:T(8,128)} %helm.1) | copy-start | bytes 1179652
